TPU v7x, 256 devices: a whole 4x4x8 slice. The times are simulated.
256 devices in a mesh: gx: 16 (over y_hi, z), gy: 4 (over x), gz: 4 (over y_lo, core).
Axes of the slice: x: 4, y: 4 (y_hi: 2, y_lo: 2; y = y_hi * 2 + y_lo), z: 8, core: 2. Of those that a mesh axis runs over, the one named last changes fastest.
Arguments:
- features: bfloat16 [32, 8, 8, 32, 128], P('gx', 'gy', 'gz'), may hold values from -6 to 6
- positions: float32 [32, 8, 8, 3, 32], P('gx', 'gy', 'gz'), may hold values from 0 to 6, as said below
- counts: int32 [32, 8, 8], P('gx', 'gy', 'gz'), may hold values from 8 to 32, as said below
- species: int32 [32, 8, 8, 32], P('gx', 'gy', 'gz'), may hold values from 0 to 4
- radial_weight: float32 [8, 3, 128], replicated, may hold values from -0.21875 to 0.21875
- mix_weight: bfloat16 [128, 128], replicated, may hold values from -0.5 to 0.5
- skip_weight: bfloat16 [5, 128, 128], replicated, may hold values from -0.5 to 0.5
- readout: float32 [5, 128], replicated, may hold values from -3 to 3
Outputs:
- new_features: bfloat16 [32, 8, 8, 32, 128], P('gx', 'gy', 'gz')
- forces: float32 [32, 8, 8, 3, 32], P('gx', 'gy', 'gz')
- feature_grad: float32 [32, 8, 8, 32, 128], P('gx', 'gy', 'gz')
Inputs may be any that keep to these rules, and one draw needn't show every extreme that they name: `counts`: some cell holds exactly 32 atoms. `positions`: coordinates lie inside the cell, atoms of one cell at least 0.6 angstroms apart.
All inputs are finite; a program needn't handle non-finite values.
Results may differ from a plain program's by a relative error of at most 0.023.
Values may be sent and summed in bfloat16 or wider, within the bound.
No kernel may reach another device: no remote copies, remote signals or barrier semaphores. Data moves between devices by JAX's collectives and lax.ppermute only.
A program may use at most 192 MiB of HBM per device.

v0:
```python
from functools import partial
import math

import jax
import jax.numpy as jnp
import numpy as np
from jax import lax
from jax.sharding import PartitionSpec as P

CUTOFF = 6.0
SENTINEL = 1000.0
SMALL = 1e-06
DEGREE = np.array([0, 1, 1, 1, 2, 2, 2, 2, 2])


def padded(x, sides, width):
    for axis, dim in sides:
        size, length = (lax.axis_size(axis), x.shape[dim])
        up = [(i, (i + 1) % size) for i in range(size)]
        down = [(j, i) for i, j in up]
        last = lax.slice_in_dim(x, length - width, length, axis=dim)
        initial = lax.slice_in_dim(x, 0, width, axis=dim)
        before = lax.ppermute(last, axis, up)
        after = lax.ppermute(initial, axis, down)
        x = jnp.concatenate([before, x, after], axis=dim)
    return x


def shortened(x):

    def short(part):
        return part.astype(jnp.bfloat16) if part.dtype == jnp.float32 else part

    return jax.tree.map(short, x)


def passed_along(value, axis, steps):
    count = lax.axis_size(axis)
    initial, last = (max(0, -steps), min(count, count - steps))
    return lax.ppermute(value, axis, [(source, source + steps) for source in range(initial, last)])


def shifted(block, axis, distance):
    devices = range(lax.axis_size(axis))
    route = [((i - distance) % len(devices), i) for i in devices]
    return lax.ppermute(block, axis, route)


def neighbour_offsets():
    shape = (3, 3, 3, 3, 1)
    first = lax.broadcasted_iota(jnp.int32, shape, 0)
    second = lax.broadcasted_iota(jnp.int32, shape, 1)
    third = lax.broadcasted_iota(jnp.int32, shape, 2)
    component = lax.broadcasted_iota(jnp.int32, shape, 3)
    picked = jnp.where(component == 0, first, jnp.where(component == 1, second, third))
    return (picked - 1).astype(jnp.float32) * CUTOFF


def cell_grid(size_x, size_y, size_z):
    flat = jnp.arange(size_x * size_y * size_z, dtype=jnp.int32)
    return jnp.stack([flat // (size_y * size_z), flat // size_z % size_y, flat % size_z], 1)


def harmonics(unit):
    unit_x, unit_y, unit_z = (unit[0], unit[1], unit[2])
    root3 = math.sqrt(3.0)
    root5 = math.sqrt(5.0)
    root15 = math.sqrt(15.0)
    return jnp.stack(
        [
            jnp.ones_like(unit_x),
            root3 * unit_x,
            root3 * unit_y,
            root3 * unit_z,
            root15 * unit_x * unit_y,
            root15 * unit_y * unit_z,
            0.5 * root5 * (3.0 * unit_z * unit_z - 1.0),
            root15 * unit_x * unit_z,
            0.5 * root15 * (unit_x * unit_x - unit_y * unit_y),
        ]
    )


def pair_table(near_pos, own_pos, nbasis):
    slots = own_pos.shape[1]
    width = near_pos.shape[1]
    delta = near_pos[:, None, :] - own_pos[:, :, None]
    radius = jnp.sqrt(jnp.sum(delta * delta, 0) + SMALL)
    unit = delta / radius
    scaled = radius / CUTOFF
    envelope = jnp.where(
        scaled < 1.0, 1.0 - 28.0 * scaled**6 + 48.0 * scaled**7 - 21.0 * scaled**8, 0.0
    )
    column = lax.broadcasted_iota(jnp.int32, (slots, width), 1)
    row_index = lax.broadcasted_iota(jnp.int32, (slots, width), 0)
    keeper = jnp.where(column == 13 * slots + row_index, 0.0, envelope)
    freqs = jnp.arange(1, nbasis + 1).astype(jnp.float32) * math.pi
    radial = (
        math.sqrt(2.0 / CUTOFF)
        * jnp.sin(freqs[:, None, None] * scaled[None])
        / radius[None]
        * keeper[None]
    )
    table = radial[:, None] * harmonics(unit)[None]
    return table.reshape(nbasis * 9 * slots, width).astype(jnp.bfloat16)


def cell_terms(
    feat_ext,
    pos_ext,
    corner,
    kinds,
    alive,
    radial_weight,
    mix_weight,
    skip_weight,
    readout,
    table_fn,
):
    slots = feat_ext.shape[3]
    chans = feat_ext.shape[4]
    nbasis = radial_weight.shape[0]
    nspecies = readout.shape[0]
    zero = jnp.zeros((), jnp.int32)
    feat_block = lax.dynamic_slice(
        feat_ext, (corner[0], corner[1], corner[2], zero, zero), (3, 3, 3, slots, chans)
    )
    pos_block = lax.dynamic_slice(
        pos_ext, (corner[0], corner[1], corner[2], zero, zero), (3, 3, 3, 3, slots)
    )
    pos_block = pos_block + neighbour_offsets()
    own_feat = feat_block[1, 1, 1].astype(jnp.bfloat16)
    near_feat = feat_block.reshape(27 * slots, chans).astype(jnp.bfloat16)
    own_pos = pos_block[1, 1, 1]
    near_pos = jnp.transpose(pos_block, (3, 0, 1, 2, 4)).reshape(3, 27 * slots)
    table = table_fn(near_pos, own_pos)
    dens = jnp.dot(table, near_feat, preferred_element_type=jnp.float32).reshape(
        nbasis, 9, slots, chans
    )
    per_comp = radial_weight[:, DEGREE, :]
    moments = jnp.einsum("bmpk,bmk->mpk", dens, per_comp, precision=lax.Precision.HIGHEST)
    product = moments[0] + jnp.sum(moments[1:4] ** 2, 0) + jnp.sum(moments[4:] ** 2, 0)
    product = product.astype(jnp.bfloat16)
    onehot = (kinds[:, None] == jnp.arange(nspecies, dtype=jnp.int32)[None, :]).astype(jnp.float32)
    updated = jnp.dot(product, mix_weight, preferred_element_type=jnp.float32)
    for kind in range(nspecies):
        updated = updated + onehot[:, kind : kind + 1] * jnp.dot(
            own_feat, skip_weight[kind], preferred_element_type=jnp.float32
        )
    chosen = jnp.dot(onehot, readout, precision=lax.Precision.HIGHEST)
    energy = jnp.sum(alive * jnp.sum(chosen * jax.nn.silu(updated), 1))
    return (energy, updated)


def place_rim(piece, dim, before, after):
    widths = [(0, 0)] * piece.ndim
    widths[dim] = (before, after)
    return jnp.pad(piece, widths)


def split_rims(arrays, dim):
    lows = tuple((lax.slice_in_dim(item, 0, 1, axis=dim) for item in arrays))
    highs = tuple(
        (lax.slice_in_dim(item, item.shape[dim] - 1, item.shape[dim], axis=dim) for item in arrays)
    )
    inners = tuple((lax.slice_in_dim(item, 1, item.shape[dim] - 1, axis=dim) for item in arrays))
    return (lows, highs, inners)


def join_rims(inners, from_below, from_above, dim):
    joined = []
    for inner, lower, upper in zip(inners, from_below, from_above):
        length = inner.shape[dim]
        joined.append(
            inner + place_rim(lower, dim, 0, length - 1) + place_rim(upper, dim, length - 1, 0)
        )
    return tuple(joined)


def shards(features, positions, counts, species, radial_weight, mix_weight, skip_weight, readout):
    size_x, size_y, size_z, slots, chans = features.shape
    nbasis = radial_weight.shape[0]
    live = (lax.broadcasted_iota(jnp.int32, counts.shape + (slots,), 3) < counts[..., None]).astype(
        jnp.float32
    )
    moved = jnp.where(live[:, :, :, None, :] > 0, positions, SENTINEL)
    feat_ext = padded(features, (("gx", 0), ("gy", 1), ("gz", 2)), 1).astype(jnp.float32)
    pos_ext = padded(moved, (("gx", 0), ("gy", 1), ("gz", 2)), 1)
    depth = size_z + 2
    layer = lax.broadcasted_iota(jnp.int32, (1, 1, depth, 1, 1), 2)
    plane = lax.axis_index("gz")
    planes = lax.axis_size("gz")
    outside = (layer == 0) & (plane == 0) | (layer == depth - 1) & (plane == planes - 1)
    grid = cell_grid(size_x, size_y, size_z)
    kinds_flat = species.reshape(-1, slots)
    alive_flat = live.reshape(-1, slots)
    table_fn = jax.checkpoint(partial(pair_table, nbasis=nbasis))

    def total(feat_all, pos_all):
        pos_all = jnp.where(outside, SENTINEL, pos_all)

        def per_cell(item):
            return cell_terms(
                feat_all,
                pos_all,
                item[0],
                item[1],
                item[2],
                radial_weight,
                mix_weight,
                skip_weight,
                readout,
                table_fn,
            )

        energies, updated = lax.map(per_cell, (grid, kinds_flat, alive_flat))
        return (jnp.sum(energies), updated)

    energy, pullback, updated = jax.vjp(total, feat_ext, pos_ext, has_aux=True)
    grad_feat, grad_pos = pullback(jnp.ones((), jnp.float32))
    lows, highs, inners = split_rims((grad_feat, grad_pos), 2)
    from_below = passed_along((shortened(highs[0]), shortened(highs[1])), "gz", 1)
    from_above = passed_along((shortened(lows[0]), shortened(lows[1])), "gz", -1)
    pair_grads = join_rims(inners, from_below, from_above, 2)
    lows, highs, inners = split_rims(pair_grads, 1)
    from_below = shifted((shortened(highs[0]), shortened(highs[1])), "gy", 1)
    from_above = shifted((shortened(lows[0]), shortened(lows[1])), "gy", -1)
    pair_grads = join_rims(inners, from_below, from_above, 1)
    lows, highs, inners = split_rims(pair_grads, 0)
    from_below = shifted((shortened(highs[0]), shortened(highs[1])), "gx", 1)
    from_above = shifted((shortened(lows[0]), shortened(lows[1])), "gx", -1)
    own_feat_grad, own_pos_grad = join_rims(inners, from_below, from_above, 0)
    new_features = (updated.reshape(size_x, size_y, size_z, slots, chans) * live[..., None]).astype(
        jnp.bfloat16
    )
    forces = -own_pos_grad * live[:, :, :, None, :]
    return (new_features, forces, own_feat_grad)


def solution(mesh):
    return jax.shard_map(
        shards,
        mesh=mesh,
        in_specs=(
            P("gx", "gy", "gz", None, None),
            P("gx", "gy", "gz", None, None),
            P("gx", "gy", "gz"),
            P("gx", "gy", "gz", None),
            P(),
            P(),
            P(),
            P(),
        ),
        out_specs=(
            P("gx", "gy", "gz", None, None),
            P("gx", "gy", "gz", None, None),
            P("gx", "gy", "gz", None, None),
        ),
        check_vma=False,
    )
```

profile of v0, /device:TPU:8, one launch (start us, length us, event | category | flops | bytes accessed | tf_op | source)
XLA Modules:
  0.0 627.5 jit_solution(4946494454996069843)
XLA Ops:
  2.1 7.7 %collective-permute-start.1 = (f32[1,2,2,3,32]{4,2,3,1,0:T(2,128)S(1)}, f32[1,2,2,3,32]{4,2,3,1,0:T(2,128)S(1)}, u32[]{:S(2)}, u32[]{:S(2)}) collective-permute-start(f32[1,2,2,3,32]{4,2,3,1,0:T(2,128)S(1)} %get-tuple-element.1793), channel_id=1, source_target_pairs={{16,0},{32,16},{48,32},{64,48},{80,64},{96,80},{112,96},{128,112},... | collective-permute-start | bytes 4616 | tf_op jit(solution)/shard_map/ppermute | solution.py:24
  10.6 5.7 collective-permute-start.7
  40.3 191.3 %while.71 = (s32[]{:T(128)}, f32[8,32,128]{2,1,0:T(8,128)S(1)}, s32[8]{0:T(128)}, s32[8]{0:T(128)}, s32[8]{0:T(128)}, /*index=5*/f32[8,3,864]{2,1,0:T(4,128)}, f...) while((s32[]{:T(128)}, f32[8,32,128]{2,1,0:T(8,128)S(1)}, ...), condition=%wide.region_4.5_spmd.clone, body=%wide.region_0.4_spmd.clone.sunk | while | flops 527070176 | bytes 23556356 | solution.py:216
  231.7 362.4 %while.70 = (s32[]{:T(128)}, f32[4,4,4,32,128]{4,3,2,1,0:T(8,128)S(1)}, f32[4,4,4,3,32]{4,2,3,1,0:T(4,128)S(1)}, s32[8]{0:T(128)}, s32[8]{0:T(128)}, /*index=5*/...) while((s32[]{:T(128)}, ...), condition=%wide.region_15.16_spmd, body=%wide.region_5.15_spmd.sunk | while | flops 1042655808 | bytes 47504740 | solution.py:216
  253.0 6.9 %copy.68 = f32[2304,864]{1,0:T(8,128)} copy(bf16[2304,864]{0,1:T(8,128)(2,1)} %convolution_convert_fusion.16) | data formatting | bytes 11943936 | tf_op jit(solution)/shard_map/transpose(jvp())/while/body/eval_jaxpr/checkpoint/reshape | solution.py:105
  263.5 4.8 multiply_reduce_fusion.8
  268.6 4.1 fusion.244
  298.2 6.9 %copy.68 = f32[2304,864]{1,0:T(8,128)} copy(bf16[2304,864]{0,1:T(8,128)(2,1)} %convolution_convert_fusion.16) | data formatting | bytes 11943936 | tf_op jit(solution)/shard_map/transpose(jvp())/while/body/eval_jaxpr/checkpoint/reshape | solution.py:105
  308.8 4.8 multiply_reduce_fusion.8
  313.9 4.1 fusion.244
  343.5 6.9 %copy.68 = f32[2304,864]{1,0:T(8,128)} copy(bf16[2304,864]{0,1:T(8,128)(2,1)} %convolution_convert_fusion.16) | data formatting | bytes 11943936 | tf_op jit(solution)/shard_map/transpose(jvp())/while/body/eval_jaxpr/checkpoint/reshape | solution.py:105
  354.1 4.8 multiply_reduce_fusion.8
  359.2 4.1 fusion.244
  384.8 4.0 convolution_convert_fusion.16
  388.8 6.9 %copy.68 = f32[2304,864]{1,0:T(8,128)} copy(bf16[2304,864]{0,1:T(8,128)(2,1)} %convolution_convert_fusion.16) | data formatting | bytes 11943936 | tf_op jit(solution)/shard_map/transpose(jvp())/while/body/eval_jaxpr/checkpoint/reshape | solution.py:105
  399.4 4.8 multiply_reduce_fusion.8
  404.5 4.1 fusion.244
  434.1 6.9 %copy.68 = f32[2304,864]{1,0:T(8,128)} copy(bf16[2304,864]{0,1:T(8,128)(2,1)} %convolution_convert_fusion.16) | data formatting | bytes 11943936 | tf_op jit(solution)/shard_map/transpose(jvp())/while/body/eval_jaxpr/checkpoint/reshape | solution.py:105
  444.7 4.8 multiply_reduce_fusion.8
  449.7 4.1 fusion.244
  479.3 6.9 %copy.68 = f32[2304,864]{1,0:T(8,128)} copy(bf16[2304,864]{0,1:T(8,128)(2,1)} %convolution_convert_fusion.16) | data formatting | bytes 11943936 | tf_op jit(solution)/shard_map/transpose(jvp())/while/body/eval_jaxpr/checkpoint/reshape | solution.py:105
  489.9 4.8 multiply_reduce_fusion.8
  495.0 4.1 fusion.244
  524.6 6.9 %copy.68 = f32[2304,864]{1,0:T(8,128)} copy(bf16[2304,864]{0,1:T(8,128)(2,1)} %convolution_convert_fusion.16) | data formatting | bytes 11943936 | tf_op jit(solution)/shard_map/transpose(jvp())/while/body/eval_jaxpr/checkpoint/reshape | solution.py:105
  535.2 4.8 multiply_reduce_fusion.8
  540.2 4.1 fusion.244
  565.9 4.0 convolution_convert_fusion.16
  569.9 6.9 %copy.68 = f32[2304,864]{1,0:T(8,128)} copy(bf16[2304,864]{0,1:T(8,128)(2,1)} %convolution_convert_fusion.16) | data formatting | bytes 11943936 | tf_op jit(solution)/shard_map/transpose(jvp())/while/body/eval_jaxpr/checkpoint/reshape | solution.py:105
  580.4 4.8 multiply_reduce_fusion.8
  585.5 4.1 fusion.244
  615.1 4.2 collective-permute-start.23
  621.3 5.5 collective-permute-done.22
  (1081 shorter events, 425.0 us)
Async XLA Ops:
  0.6 22.4 %copy-start = (f32[8,3,128]{2,0,1:T(8,128)S(1)}, f32[8,3,128]{2,0,1:T(8,128)}, u32[]{:S(2)}) copy-start(f32[8,3,128]{2,0,1:T(8,128)} %param.18) | copy-start | bytes 36868
  2.1 17.8 %collective-permute-start.1 = (f32[1,2,2,3,32]{4,2,3,1,0:T(2,128)S(1)}, f32[1,2,2,3,32]{4,2,3,1,0:T(2,128)S(1)}, u32[]{:S(2)}, u32[]{:S(2)}) collective-permute-start(f32[1,2,2,3,32]{4,2,3,1,0:T(2,128)S(1)} %get-tuple-element.1793), channel_id=1, source_target_pairs={{16,0},{32,16},{48,32},{64,48},{80,64},{96,80},{112,96},{128,112},... | collective-permute-start | bytes 4616 | tf_op jit(solution)/shard_map/ppermute | solution.py:24
  9.8 10.1 %collective-permute-start = (f32[1,2,2,3,32]{4,2,3,1,0:T(2,128)S(1)}, f32[1,2,2,3,32]{4,2,3,1,0:T(2,128)S(1)}, u32[]{:S(2)}, u32[]{:S(2)}) collective-permute-start(f32[1,2,2,3,32]{4,2,3,1,0:T(2,128)S(1)} %get-tuple-element.1792), channel_id=1, source_target_pairs={{0,16},{16,32},{32,48},{48,64},{64,80},{80,96},{96,112},{112,128},... | collective-permute-start | bytes 4616 | tf_op jit(solution)/shard_map/ppermute | solution.py:23
  10.6 17.2 %collective-permute-start.6 = (bf16[1,2,2,32,128]{4,3,2,1,0:T(8,128)(2,1)S(1)}, bf16[1,2,2,32,128]{4,3,2,1,0:T(8,128)(2,1)S(1)}, u32[]{:S(2)}, u32[]{:S(2)}) collective-permute-start(bf16[1,2,2,32,128]{4,3,2,1,0:T(8,128)(2,1)S(1)} %get-tuple-element.1781), channel_id=1, source_target_pairs={{0,16},{16,32},{32,48},{48,64},{64,80},{80,96},{96,112},{112,128},... | collective-permute-start | bytes 98312 | tf_op jit(solution)/shard_map/ppermute | solution.py:23
  10.6 18.1 %collective-permute-start.7 = (bf16[1,2,2,32,128]{4,3,2,1,0:T(8,128)(2,1)S(1)}, bf16[1,2,2,32,128]{4,3,2,1,0:T(8,128)(2,1)S(1)}, u32[]{:S(2)}, u32[]{:S(2)}) collective-permute-start(bf16[1,2,2,32,128]{4,3,2,1,0:T(8,128)(2,1)S(1)} %get-tuple-element.1780), channel_id=1, source_target_pairs={{16,0},{32,16},{48,32},{64,48},{80,64},{96,80},{112,96},{128,112},... | collective-permute-start | bytes 98312 | tf_op jit(solution)/shard_map/ppermute | solution.py:24
  20.0 4.2 collective-permute-start.3
  22.8 4.9 collective-permute-start.2
  22.8 17.4 %copy-start.12 = (pred[4]{0:T(512)(128)(4,1)}, pred[4]{0:T(512)(128)(4,1)S(1)}, u32[]{:S(2)}) copy-start(pred[4]{0:T(512)(128)(4,1)S(1)} %and_or_fusion) | copy-start | bytes 16
  28.7 4.3 collective-permute-start.9
  28.8 5.6 collective-permute-start.8
  30.8 4.2 collective-permute-start.5
  30.9 4.1 collective-permute-start.4
  34.4 2.9 collective-permute-start.11
  34.5 5.7 collective-permute-start.10
  231.7 362.4 %copy-start.13 = (pred[4]{0:T(512)(128)(4,1)S(1)}, pred[4]{0:T(512)(128)(4,1)}, u32[]{:S(2)}) copy-start(pred[4]{0:T(512)(128)(4,1)} %copy-done.12) | copy-start | bytes 16
  231.9 13.1 %copy-start.5 = (bf16[128,128]{1,0:T(8,128)(2,1)S(1)}, bf16[128,128]{1,0:T(8,128)(2,1)}, u32[]{:S(2)}) copy-start(bf16[128,128]{1,0:T(8,128)(2,1)} %get-tuple-element.2458) | copy-start | bytes 98308 | tf_op jit(solution)/shard_map/transpose(jvp())/while
  277.2 13.1 %copy-start.5 = (bf16[128,128]{1,0:T(8,128)(2,1)S(1)}, bf16[128,128]{1,0:T(8,128)(2,1)}, u32[]{:S(2)}) copy-start(bf16[128,128]{1,0:T(8,128)(2,1)} %get-tuple-element.2458) | copy-start | bytes 98308 | tf_op jit(solution)/shard_map/transpose(jvp())/while
  367.8 13.1 %copy-start.5 = (bf16[128,128]{1,0:T(8,128)(2,1)S(1)}, bf16[128,128]{1,0:T(8,128)(2,1)}, u32[]{:S(2)}) copy-start(bf16[128,128]{1,0:T(8,128)(2,1)} %get-tuple-element.2458) | copy-start | bytes 98308 | tf_op jit(solution)/shard_map/transpose(jvp())/while
  548.8 13.1 %copy-start.5 = (bf16[128,128]{1,0:T(8,128)(2,1)S(1)}, bf16[128,128]{1,0:T(8,128)(2,1)}, u32[]{:S(2)}) copy-start(bf16[128,128]{1,0:T(8,128)(2,1)} %get-tuple-element.2458) | copy-start | bytes 98308 | tf_op jit(solution)/shard_map/transpose(jvp())/while
  594.1 33.4 %copy-start.1 = (f32[8,3,128]{2,0,1:T(8,128)S(1)}, f32[8,3,128]{2,0,1:T(8,128)}, u32[]{:S(2)}) copy-start(f32[8,3,128]{2,0,1:T(8,128)} %param.18) | copy-start | bytes 36868
  594.3 9.6 %collective-permute-start.13 = (bf16[4,4,1,3,32]{4,2,3,1,0:T(2,128)(2,1)S(1)}, bf16[4,4,1,3,32]{4,2,3,1,0:T(2,128)(2,1)S(1)}, u32[]{:S(2)}, u32[]{:S(2)}) collective-permute-start(bf16[4,4,1,3,32]{4,2,3,1,0:T(2,128)(2,1)S(1)} %get-tuple-element.1783), channel_id=1, source_target_pairs={{1,0},{2,1},{3,2},{5,4},{6,5},{7,6},{9,8},{10,9},{11,10},{13,12},{... | collective-permute-start | bytes 9224 | tf_op jit(solution)/shard_map/ppermute | solution.py:40
  596.2 7.7 %collective-permute-start.12 = (bf16[4,4,1,3,32]{4,2,3,1,0:T(2,128)(2,1)S(1)}, bf16[4,4,1,3,32]{4,2,3,1,0:T(2,128)(2,1)S(1)}, u32[]{:S(2)}, u32[]{:S(2)}) collective-permute-start(bf16[4,4,1,3,32]{4,2,3,1,0:T(2,128)(2,1)S(1)} %get-tuple-element.1782), channel_id=1, source_target_pairs={{0,1},{1,2},{2,3},{4,5},{5,6},{6,7},{8,9},{9,10},{10,11},{12,13},{... | collective-permute-start | bytes 9224 | tf_op jit(solution)/shard_map/ppermute | solution.py:40
  598.7 10.5 %collective-permute-start.19 = (bf16[4,4,1,32,128]{4,3,2,1,0:T(8,128)(2,1)S(1)}, bf16[4,4,1,32,128]{4,3,2,1,0:T(8,128)(2,1)S(1)}, u32[]{:S(2)}, u32[]{:S(2)}) collective-permute-start(bf16[4,4,1,32,128]{4,3,2,1,0:T(8,128)(2,1)S(1)} %get-tuple-element.1766), channel_id=1, source_target_pairs={{1,0},{2,1},{3,2},{5,4},{6,5},{7,6},{9,8},{10,9},{11,10},{13,12},{... | collective-permute-start | bytes 393224 | tf_op jit(solution)/shard_map/ppermute | solution.py:40
  601.9 7.4 %collective-permute-start.18 = (bf16[4,4,1,32,128]{4,3,2,1,0:T(8,128)(2,1)S(1)}, bf16[4,4,1,32,128]{4,3,2,1,0:T(8,128)(2,1)S(1)}, u32[]{:S(2)}, u32[]{:S(2)}) collective-permute-start(bf16[4,4,1,32,128]{4,3,2,1,0:T(8,128)(2,1)S(1)} %get-tuple-element.1765), channel_id=1, source_target_pairs={{0,1},{1,2},{2,3},{4,5},{5,6},{6,7},{8,9},{9,10},{10,11},{12,13},{... | collective-permute-start | bytes 393224 | tf_op jit(solution)/shard_map/ppermute | solution.py:40
  604.0 3.7 collective-permute-start.15
  604.1 5.2 collective-permute-start.14
  609.4 4.3 collective-permute-start.21
  609.5 5.6 collective-permute-start.20
  611.5 7.8 %collective-permute-start.17 = (bf16[1,2,2,3,32]{4,2,3,1,0:T(2,128)(2,1)S(1)}, bf16[1,2,2,3,32]{4,2,3,1,0:T(2,128)(2,1)S(1)}, u32[]{:S(2)}, u32[]{:S(2)}) collective-permute-start(bf16[1,2,2,3,32]{4,2,3,1,0:T(2,128)(2,1)S(1)} %get-tuple-element.1791), channel_id=1, source_target_pairs={{16,0},{32,16},{48,32},{64,48},{80,64},{96,80},{112,96},{128,112},... | collective-permute-start | bytes 2312 | tf_op jit(solution)/shard_map/ppermute | solution.py:46
  613.5 7.2 %collective-permute-start.16 = (bf16[1,2,2,3,32]{4,2,3,1,0:T(2,128)(2,1)S(1)}, bf16[1,2,2,3,32]{4,2,3,1,0:T(2,128)(2,1)S(1)}, u32[]{:S(2)}, u32[]{:S(2)}) collective-permute-start(bf16[1,2,2,3,32]{4,2,3,1,0:T(2,128)(2,1)S(1)} %get-tuple-element.1790), channel_id=1, source_target_pairs={{240,0},{0,16},{16,32},{32,48},{48,64},{64,80},{80,96},{96,112},{1... | collective-permute-start | bytes 2312 | tf_op jit(solution)/shard_map/ppermute | solution.py:46
  615.1 6.2 collective-permute-start.23
  619.3 7.5 %collective-permute-start.22 = (bf16[1,2,2,32,128]{4,3,2,1,0:T(8,128)(2,1)S(1)}, bf16[1,2,2,32,128]{4,3,2,1,0:T(8,128)(2,1)S(1)}, u32[]{:S(2)}, u32[]{:S(2)}) collective-permute-start(bf16[1,2,2,32,128]{4,3,2,1,0:T(8,128)(2,1)S(1)} %get-tuple-element.1776), channel_id=1, source_target_pairs={{240,0},{0,16},{16,32},{32,48},{48,64},{64,80},{80,96},{96,112},{1... | collective-permute-start | bytes 98312 | tf_op jit(solution)/shard_map/ppermute | solution.py:46
  (76 other events, 580.5 us)
where the time goes:
time: 635 us; the launch traced here: 628 us
  local copies, waits for them, and re-layouts  213 us (34%)
  other arithmetic  210 us (33%)
  matrix products  97.5 us (15%)
  loops' own time  44.1 us (7%)
  starting transfers between devices  39.3 us (6%)
  waiting for transfers between devices  23 us (4%)
    dot_general x24, matrix products, cell_terms(): jnp.dot(table, near_feat, preferred_element_type=jnp.float32)  70.3 us
    dynamic_update_slice x64, local copies, waits for them, and re-layouts, total(): energies, updated = lax.map(per_cell, (grid, kinds_flat, alive_flat))  63.7 us
    reshape x8, local copies, waits for them, and re-layouts, pair_table(): return table.reshape(nbasis * 9 * slots, width).astype(jnp.bfloat16)  55.2 us
    mul x16, other arithmetic, pair_table(): math.sqrt(2.0 / CUTOFF) * jnp.sin(freqs[:, None, None] * scaled[None])  49.5 us
    another operation x2, loops' own time, total(): energies, updated = lax.map(per_cell, (grid, kinds_flat, alive_flat))  44.1 us
    reduce_sum x8, other arithmetic, pair_table(): table = radial[:, None] * harmonics(unit)[None]  38.5 us
    reduce_sum x8, other arithmetic, pair_table(): math.sqrt(2.0 / CUTOFF) * jnp.sin(freqs[:, None, None] * scaled[None])  32.4 us
    dynamic_slice x48, local copies, waits for them, and re-layouts, total(): energies, updated = lax.map(per_cell, (grid, kinds_flat, alive_flat))  30.3 us
  transfers between devices with their start and end apart: 24, of which 12 were waited for; matrix products, arithmetic and copies ran while one was open for 1% of the time, Pallas kernels for 0%

commit v1 on v0

v1 whole, which is shorter than its diff:
```python
from functools import partial
import math

import jax
import jax.numpy as jnp
from jax import lax
from jax.experimental import pallas as pl
from jax.experimental.pallas import tpu as pltpu
from jax.sharding import PartitionSpec as P

CUTOFF = 6.0
SENTINEL = 1000.0
SMALL = 1e-06
K = 128
NB = 8
NM = 9
SPECIES = 5
SLOTS = 32
CELLS = 8
DEG = (0, 1, 1, 1, 2, 2, 2, 2, 2)
OWN = CELLS * SLOTS
GHOSTS = 19
GWIDTH = 640
ROW = SLOTS + 16
HALF = NB * NM * 16
ROWS = 2 * HALF
F32 = jnp.float32
BF16 = jnp.bfloat16
ROOT3, ROOT5, ROOT15 = math.sqrt(3.0), math.sqrt(5.0), math.sqrt(15.0)
NORM = math.sqrt(2.0 / CUTOFF)
COS_FIT = (3.999999997, -3.739208102, 1.277990829, -0.2287452958, 0.02416752431)
SIN_FIT = (3.141592654, -5.167712765, 2.550163319, -0.5992521978, 0.08205040168, -0.00702838621)
GHOST_LIST = tuple(
    (a, b, c) for a in range(3) for b in range(3) for c in range(3) if 2 in (a, b, c)
)


def horner(coefs, y):
    acc = jnp.full_like(y, coefs[-1])
    for value in coefs[-2::-1]:
        acc = acc * y + value
    return acc


def pair_geometry(near, own, self_lane):
    dx, dy, dz = (near[k] - own[k] for k in range(3))
    inv = lax.rsqrt(dx * dx + dy * dy + dz * dz + SMALL)
    r2 = dx * dx + dy * dy + dz * dz + SMALL
    s = jnp.minimum(r2 * inv * (1.0 / CUTOFF), 1.0)
    ux, uy, uz = dx * inv, dy * inv, dz * inv
    t = 0.5 - s
    y = t * t
    first = (1.0 - s) * horner(COS_FIT, y) * (NORM / CUTOFF)
    cosine = t * horner(SIN_FIT, y)
    s2 = s * s
    s5 = s2 * s2 * s
    env = 1.0 - s5 * s * (28.0 - 48.0 * s + 21.0 * s2)
    away = 1.0 - s
    denv = s5 * (away * away) * (-168.0 / CUTOFF)
    if self_lane is not None:
        lane = lax.broadcasted_iota(jnp.int32, dx.shape, 1)
        row = lax.broadcasted_iota(jnp.int32, dx.shape, 0)
        same = lane == row + self_lane
        env = jnp.where(same, 0.0, env)
        denv = jnp.where(same, 0.0, denv)
    return inv, ux, uy, uz, first, cosine, env, denv


def sine_series(first, cosine):
    twice = cosine + cosine
    out = [first, twice * first]
    for _ in range(NB - 2):
        out.append(twice * out[-1] - out[-2])
    return out


def cosine_series(cosine):
    twice = cosine + cosine
    out = [cosine, twice * cosine - 1.0]
    for _ in range(NB - 2):
        out.append(twice * out[-1] - out[-2])
    return [float(b + 1) * value for b, value in enumerate(out)]


def harmonics(ux, uy, uz):
    return [
        None,
        ROOT3 * ux,
        ROOT3 * uy,
        ROOT3 * uz,
        ROOT15 * ux * uy,
        ROOT15 * uy * uz,
        0.5 * ROOT5 * (3.0 * uz * uz - 1.0),
        ROOT15 * ux * uz,
        0.5 * ROOT15 * (ux * ux - uy * uy),
    ]


def lane_to_rows(line):
    return jnp.broadcast_to(line, (128, 128)).T


def contract_last(a, b):
    return lax.dot_general(a, b, (((1,), (1,)), ((), ())), preferred_element_type=F32)


def flat(x, y, z):
    return x * 16 + y * 4 + z


def own_xyz(cell):
    return cell // 4, (cell // 2) % 2, cell % 2


def tail_of(rows):
    index = lax.broadcasted_iota(jnp.int32, (16, 128), 0)
    tail = jnp.zeros((16, 128), F32)
    for k, line in enumerate(rows):
        tail = jnp.where(index == k, jnp.broadcast_to(line, (16, 128)), tail)
    return tail.astype(BF16)


def split_line(line, pieces):
    out = []
    for _ in range(pieces):
        part = line.astype(BF16).astype(F32)
        out.append(part)
        line = line - part
    return out


def line_of(ref, cell, pieces):
    tail = ref[cell, SLOTS:ROW, :].astype(F32)
    line = tail[0:1, :]
    for k in range(1, pieces):
        line = line + tail[k : k + 1, :]
    return line


def ext_source(x, y, z, own, xlo, xhi, ylo, yhi, zlo, zhi):
    if z in (0, 3):
        return (zlo if z == 0 else zhi), x * 4 + y
    if y in (0, 3):
        return (ylo if y == 0 else yhi), x * 2 + z - 1
    if x in (0, 3):
        return (xlo if x == 0 else xhi), (y - 1) * 2 + z - 1
    return own, (x - 1) * 4 + (y - 1) * 2 + z - 1


def pack_x_kernel(counts_ref, feat_ref, pos_ref, own_ref, xlo_ref, xhi_ref, line_ref):
    lane = lax.broadcasted_iota(jnp.int32, (1, SLOTS), 1)
    line_ref[...] = jnp.zeros_like(line_ref)
    for c in range(CELLS):
        for k in range(3):
            x, y, z = own_xyz(c)
            value = pos_ref[x, y, k, z : z + 1, :]
            value = jnp.where(lane < counts_ref[x, y, z], value, SENTINEL)
            line_ref[c : c + 1, k * SLOTS : (k + 1) * SLOTS] = value
    pieces = split_line(line_ref[...], 3)
    for c in range(CELLS):
        tail = tail_of([piece[c : c + 1, :] for piece in pieces])
        feat = feat_ref[c]
        for ref, spot in ((own_ref, c), ((xlo_ref, xhi_ref)[c // 4], c % 4)):
            ref[spot, 0:SLOTS, :] = feat
            ref[spot, SLOTS:ROW, :] = tail


def pack_y_kernel(own, xlo, xhi, lo_ref, hi_ref):
    for y, ref in ((1, lo_ref), (2, hi_ref)):
        for x in range(4):
            for z in (1, 2):
                source, spot = ext_source(x, y, z, own, xlo, xhi, None, None, None, None)
                ref[x * 2 + z - 1] = source[spot]


def pack_z_kernel(own, xlo, xhi, ylo, yhi, lo_ref, hi_ref):
    for z, ref in ((1, lo_ref), (2, hi_ref)):
        for x in range(4):
            for y in range(4):
                source, spot = ext_source(x, y, z, own, xlo, xhi, ylo, yhi, None, None)
                ref[x * 4 + y] = source[spot]


def load_own(own_ref, nf_ref, near_ref, ownpos_ref):
    for c in range(CELLS):
        nf_ref[c * SLOTS : (c + 1) * SLOTS, :] = own_ref[c, 0:SLOTS, :]
        line = line_of(own_ref, c, 3)
        for k, spot in enumerate(own_xyz(c)):
            moved = line[:, k * SLOTS : (k + 1) * SLOTS] + (spot + 1) * CUTOFF
            near_ref[k : k + 1, c * SLOTS : (c + 1) * SLOTS] = moved
    for half in range(2):
        lanes = slice(half * 128, half * 128 + 128)
        for k in range(3):
            ownpos_ref[k, lanes, :] = lane_to_rows(near_ref[k : k + 1, lanes])


def geometry_of(near_ref, ownpos_ref, cell, block, tile, own_pairs):
    lanes = slice(tile * 128, tile * 128 + 128)
    near = [near_ref[k : k + 1, lanes] for k in range(3)]
    start = pl.multiple_of(cell * SLOTS + block * 16, 16)
    own = [ownpos_ref[k, pl.ds(start, 16), :] for k in range(3)]
    return pair_geometry(near, own, start - tile * 128 if own_pairs else None)


def build_table(table_ref, geometry, tiles):
    for tile in range(tiles):
        lanes = slice(tile * 128, tile * 128 + 128)
        for block in range(2):
            inv, ux, uy, uz, first, cosine, env, denv = geometry(block, tile)
            radial = [value * env for value in sine_series(first, cosine)]
            shape = harmonics(ux, uy, uz)
            for b in range(NB):
                for m in range(NM):
                    row = block * HALF + (b * NM + m) * 16
                    value = radial[b] if m == 0 else radial[b] * shape[m]
                    table_ref[row : row + 16, lanes] = value.astype(BF16)


def weigh(dens_ref, rw_ref, block, m):
    total = None
    for b in range(NB):
        row = block * HALF + (b * NM + m) * 16
        weight = rw_ref[DEG[m], b : b + 1, :]
        term = dens_ref[row : row + 16, :] * weight
        total = term if total is None else total + term
    return total


def spread(mom_ref, cell, rw_ref, dd_ref):
    for block in range(2):
        for m in range(NM):
            cot = mom_ref[cell, m, block * 16 : block * 16 + 16, :]
            for b in range(NB):
                row = block * HALF + (b * NM + m) * 16
                weight = rw_ref[DEG[m], b : b + 1, :]
                dd_ref[row : row + 16, :] = (cot * weight).astype(BF16)


def pair_forces(geometry, dd_ref, nf_ref, dt_ref, width, near_out, fown_ref):
    pulls = [[None] * 3, [None] * 3]
    for chunk in range((width + 255) // 256):
        low = chunk * 256
        high = min(low + 256, width)
        slab = dt_ref.at[chunk % 2]
        slab[:, : high - low] = contract_last(dd_ref[...], nf_ref[low:high, :])
        for tile in range(low // 128, high // 128):
            inside = slice(tile * 128 - low, tile * 128 - low + 128)
            near_sum = [None] * 3
            for block in range(2):
                inv, ux, uy, uz, first, cosine, env, denv = geometry(block, tile)
                sines = sine_series(first, cosine)
                cosines = cosine_series(cosine)
                shape = harmonics(ux, uy, uz)
                pull = [None] * NM
                total_s = None
                total_c = None
                for m in range(NM):
                    part_s = None
                    part_c = None
                    for b in range(NB):
                        row = block * HALF + (b * NM + m) * 16
                        value = slab[row : row + 16, inside]
                        one, two = value * sines[b], value * cosines[b]
                        part_s = one if part_s is None else part_s + one
                        part_c = two if part_c is None else part_c + two
                    pull[m] = part_s
                    if m == 0:
                        total_s, total_c = part_s, part_c
                    else:
                        total_s = total_s + part_s * shape[m]
                        total_c = total_c + part_c * shape[m]
                gx = ROOT3 * pull[1] + ROOT15 * (uy * pull[4] + uz * pull[7] + ux * pull[8])
                gy = ROOT3 * pull[2] + ROOT15 * (ux * pull[4] + uz * pull[5] - uy * pull[8])
                gz = (
                    ROOT3 * pull[3]
                    + ROOT15 * (uy * pull[5] + ux * pull[7])
                    + (3.0 * ROOT5) * uz * pull[6]
                )
                scale = env * inv
                turn = ux * gx + uy * gy + uz * gz
                wave = (math.pi / CUTOFF * NORM) * total_c
                along = denv * total_s + scale * (wave - total_s - turn)
                for k, (unit, side) in enumerate(((ux, gx), (uy, gy), (uz, gz))):
                    force = unit * along + scale * side
                    near_sum[k] = force if block == 0 else near_sum[k] + force
                    held = pulls[block][k]
                    pulls[block][k] = force if held is None else held + force
            near_out(tile, [jnp.sum(value, axis=0, keepdims=True) for value in near_sum])
    for k in range(3):
        for block in range(2):
            fown_ref[k * SLOTS + block * 16 : k * SLOTS + block * 16 + 16, :] = pulls[block][k]
    return jnp.sum(fown_ref[...].T, axis=0, keepdims=True)


def own_forward_kernel(first, own_ref, rw_ref, mom_ref, nf_ref, near_ref, ownpos_ref, table_ref, dens_ref):
    load_own(own_ref, nf_ref, near_ref, ownpos_ref)

    def step(at, carry):
        cell = first + at
        build_table(table_ref, lambda b, t: geometry_of(near_ref, ownpos_ref, cell, b, t, True), 2)
        dens_ref[...] = jnp.dot(table_ref[...], nf_ref[...], preferred_element_type=F32)
        for block in range(2):
            for m in range(NM):
                mom_ref[at, m, block * 16 : block * 16 + 16, :] = weigh(dens_ref, rw_ref, block, m)
        return carry

    lax.fori_loop(0, mom_ref.shape[0], step, 0)


def own_backward_kernel(
    first, count, own_ref, rw_ref, mom_ref, gown_ref, lines_ref,
    nf_ref, near_ref, ownpos_ref, table_ref, dd_ref, dt_ref, gnear_ref, fown_ref, gsum_ref,
):
    load_own(own_ref, nf_ref, near_ref, ownpos_ref)
    gsum_ref[...] = jnp.zeros_like(gsum_ref)
    gnear_ref[...] = jnp.zeros_like(gnear_ref)
    fown_ref[...] = jnp.zeros_like(fown_ref)
    lines_ref[...] = jnp.zeros_like(lines_ref)

    def near_out(tile, sums):
        for k in range(3):
            gnear_ref[k : k + 1, tile * 128 : tile * 128 + 128] += sums[k]

    def step(at, carry):
        cell = first + at

        def geometry(block, tile):
            return geometry_of(near_ref, ownpos_ref, cell, block, tile, True)

        spread(mom_ref, cell, rw_ref, dd_ref)
        build_table(table_ref, geometry, 2)
        gsum_ref[...] += lax.dot_general(
            dd_ref[...], table_ref[...], (((0,), (0,)), ((), ())), preferred_element_type=F32
        )
        line = pair_forces(geometry, dd_ref, nf_ref, dt_ref, OWN, near_out, fown_ref)
        lines_ref[pl.ds(cell, 1), :] = -line
        return carry

    lax.fori_loop(0, count, step, 0)
    gown_ref[...] = gsum_ref[...].T
    for c in range(CELLS):
        for k in range(3):
            lanes = slice(k * SLOTS, (k + 1) * SLOTS)
            lines_ref[c : c + 1, lanes] += gnear_ref[k : k + 1, c * SLOTS : (c + 1) * SLOTS]


def ghost_kernel(
    parts, *refs
):
    counts_ref, edges_ref, own, xlo, xhi, ylo, yhi, zlo, zhi = refs[:9]
    refs = refs[1:]
    mom_in = refs[8 : 8 + parts]
    species_ref, rw_ref, mix_ref, skip_ref, readout_ref = refs[8 + parts : 13 + parts]
    new_ref, szlo, szhi, rest_ref, rlines_ref, cot_ref = refs[13 + parts : 19 + parts]
    (
        feat_ref, pos_ref, lines_ref, nf_ref, near_ref, ownnf_ref, ownnear_ref, ownpos_ref, kind_ref,
        table_ref, dens_ref, mom_ref, dd_ref, dt_ref, gnear_ref, fown_ref, gfeat_ref, gpos_ref, sline_ref, oline_ref,
    ) = refs[19 + parts :]
    load_own(own, ownnf_ref, ownnear_ref, ownpos_ref)
    for c in range(CELLS):
        sline_ref[0:1, c * SLOTS : (c + 1) * SLOTS] = species_ref[c : c + 1, :].astype(F32)
    for half in range(2):
        lanes = slice(half * 128, half * 128 + 128)
        kind_ref[lanes, :] = lane_to_rows(sline_ref[0:1, lanes])
    for x in range(4):
        for y in range(4):
            for z in range(4):
                source, spot = ext_source(x, y, z, own, xlo, xhi, ylo, yhi, zlo, zhi)
                cell = flat(x, y, z)
                feat_ref[cell] = source[spot, 0:SLOTS, :]
                lines_ref[cell : cell + 1, :] = line_of(source, spot, 3)
    index = lax.broadcasted_iota(jnp.int32, (64, SLOTS), 0)
    spots = (index >> 4, (index >> 2) & 3, index & 3)
    depth = spots[2]
    outside = ((depth == 0) & (edges_ref[0] > 0)) | ((depth == 3) & (edges_ref[1] > 0))
    for k in range(3):
        value = jnp.where(outside, SENTINEL, lines_ref[:, k * SLOTS : (k + 1) * SLOTS])
        pos_ref[k, :, 0:SLOTS] = value + spots[k].astype(F32) * CUTOFF
    spare = GWIDTH - GHOSTS * SLOTS
    near_ref[:, GHOSTS * SLOTS :] = jnp.full((8, spare), 5000.0, F32)
    nf_ref[GHOSTS * SLOTS :, :] = jnp.zeros((spare, K), BF16)
    gnear_ref[...] = jnp.zeros_like(gnear_ref)
    gfeat_ref[...] = jnp.zeros_like(gfeat_ref)
    gpos_ref[...] = jnp.zeros_like(gpos_ref)
    fown_ref[...] = jnp.zeros_like(fown_ref)
    oline_ref[...] = jnp.zeros_like(oline_ref)

    def ghost_cell(cell, which):
        return flat(*(3 * at if side == 2 else side + 1 for side, at in zip(which, own_xyz(cell))))

    def load_ghosts(cell):
        for g, which in enumerate(GHOST_LIST):
            spot = ghost_cell(cell, which)
            nf_ref[g * SLOTS : (g + 1) * SLOTS, :] = feat_ref[spot]
            for k in range(3):
                near_ref[k : k + 1, g * SLOTS : (g + 1) * SLOTS] = pos_ref[k, pl.ds(spot, 1), 0:SLOTS]

    def geometry_at(cell):
        return lambda block, tile: geometry_of(near_ref, ownpos_ref, cell, block, tile, False)

    at = 0
    for held in mom_in:
        mom_ref[at : at + held.shape[0]] = held[...]
        at += held.shape[0]

    def forward(cell, carry):
        load_ghosts(cell)
        build_table(table_ref.at[cell], geometry_at(cell), GWIDTH // 128)
        dens_ref[...] = jnp.dot(table_ref[cell], nf_ref[...], preferred_element_type=F32)
        for block in range(2):
            for m in range(NM):
                mom_ref[cell, m, block * 16 : block * 16 + 16, :] += weigh(dens_ref, rw_ref, block, m)
        return carry

    lax.fori_loop(0, CELLS, forward, 0)

    moments = [mom_ref[:, m].reshape(OWN, K) for m in range(NM)]
    product = moments[0]
    for m in range(1, NM):
        product = product + moments[m] * moments[m]
    own_feat = ownnf_ref[...]
    kinds = kind_ref[...]
    updated = jnp.dot(product.astype(BF16), mix_ref[...], preferred_element_type=F32)
    chosen = jnp.zeros((OWN, K), F32)
    for k in range(SPECIES):
        hot = kinds == float(k)
        masked = jnp.where(hot, own_feat.astype(F32), 0.0).astype(BF16)
        updated = updated + jnp.dot(masked, skip_ref[k], preferred_element_type=F32)
        chosen = jnp.where(hot, readout_ref[k : k + 1, :], chosen)
    slot = lax.broadcasted_iota(jnp.int32, (SLOTS, K), 0)
    alive = jnp.concatenate(
        [jnp.where(slot < counts_ref[own_xyz(c)], 1.0, 0.0) for c in range(CELLS)], axis=0
    )
    new_ref[...] = (updated * alive).astype(BF16)
    gate = 1.0 / (1.0 + jnp.exp(-updated))
    dupdated = alive * chosen * gate * (1.0 + updated * (1.0 - gate))
    dproduct = contract_last(dupdated.astype(BF16), mix_ref[...])
    dskip = jnp.zeros((OWN, K), F32)
    for k in range(SPECIES):
        masked = jnp.where(kinds == float(k), dupdated, 0.0).astype(BF16)
        dskip = dskip + contract_last(masked, skip_ref[k])
    for c in range(CELLS):
        x, y, z = own_xyz(c)
        gfeat_ref[flat(x + 1, y + 1, z + 1)] = dskip[c * SLOTS : (c + 1) * SLOTS, :]
    cot_ref[:, 0] = dproduct.reshape(CELLS, SLOTS, K)
    for m in range(1, NM):
        cot_ref[:, m] = (2.0 * moments[m] * dproduct).reshape(CELLS, SLOTS, K)

    def near_out(tile, sums):
        for k in range(3):
            gnear_ref[k : k + 1, tile * 128 : tile * 128 + 128] = sums[k]

    def backward(cell, carry):
        load_ghosts(cell)
        spread(cot_ref, cell, rw_ref, dd_ref)
        grads = lax.dot_general(
            dd_ref[...], table_ref[cell], (((0,), (0,)), ((), ())), preferred_element_type=F32
        ).T
        for g, which in enumerate(GHOST_LIST):
            gfeat_ref[ghost_cell(cell, which)] += grads[g * SLOTS : (g + 1) * SLOTS, :]
        line = pair_forces(geometry_at(cell), dd_ref, nf_ref, dt_ref, GWIDTH, near_out, fown_ref)
        oline_ref[pl.ds(cell, 1), :] = -line
        for g, which in enumerate(GHOST_LIST):
            spot = ghost_cell(cell, which)
            for k in range(3):
                gpos_ref[k, pl.ds(spot, 1), 0:SLOTS] += gnear_ref[
                    k : k + 1, g * SLOTS : (g + 1) * SLOTS
                ]
        return carry

    lax.fori_loop(0, CELLS, backward, 0)

    for k in range(3):
        lines_ref[:, k * SLOTS : (k + 1) * SLOTS] = gpos_ref[k, :, 0:SLOTS]
    for c in range(CELLS):
        cell = flat(*(at + 1 for at in own_xyz(c)))
        lines_ref[cell : cell + 1, :] = oline_ref[c : c + 1, :]
    pieces = split_line(lines_ref[...], 2)
    for x in range(4):
        for y in range(4):
            for z in (1, 2):
                at, cell = (x * 4 + y) * 2 + z - 1, flat(x, y, z)
                rest_ref[at] = gfeat_ref[cell]
                rlines_ref[at : at + 1, :] = lines_ref[cell : cell + 1, :]
            for z, ref in ((0, szlo), (3, szhi)):
                at, cell = x * 4 + y, flat(x, y, z)
                ref[at, 0:SLOTS, :] = gfeat_ref[cell].astype(BF16)
                ref[at, SLOTS:ROW, :] = tail_of([piece[cell : cell + 1, :] for piece in pieces])


def gathered(x, y, z, rest_ref, rlines_ref, zs, ys, xs):
    at = (x * 4 + y) * 2 + z - 1
    feat = rest_ref[at]
    line = rlines_ref[at : at + 1, :]
    for faces, side, spot in (
        (zs, z, x * 4 + y),
        (ys, y, x * 2 + z - 1),
        (xs, x, (y - 1) * 2 + z - 1),
    ):
        if faces is not None:
            ref = faces[side - 1]
            feat = feat + ref[spot, 0:SLOTS, :].astype(F32)
            line = line + line_of(ref, spot, 2)
    return feat, line


def back_y_kernel(rest_ref, rlines_ref, zlo, zhi, lo_ref, hi_ref):
    for y, ref in ((0, lo_ref), (3, hi_ref)):
        for x in range(4):
            for z in (1, 2):
                feat, line = gathered(x, y, z, rest_ref, rlines_ref, (zlo, zhi), None, None)
                spot = x * 2 + z - 1
                ref[spot, 0:SLOTS, :] = feat.astype(BF16)
                ref[spot, SLOTS:ROW, :] = tail_of(split_line(line, 2))


def back_x_kernel(rest_ref, rlines_ref, zlo, zhi, ylo, yhi, lo_ref, hi_ref):
    for x, ref in ((0, lo_ref), (3, hi_ref)):
        for y in (1, 2):
            for z in (1, 2):
                feat, line = gathered(x, y, z, rest_ref, rlines_ref, (zlo, zhi), (ylo, yhi), None)
                spot = (y - 1) * 2 + z - 1
                ref[spot, 0:SLOTS, :] = feat.astype(BF16)
                ref[spot, SLOTS:ROW, :] = tail_of(split_line(line, 2))


def finish_kernel(parts, *refs):
    counts_ref, rest_ref, rlines_ref, zlo, zhi, ylo, yhi, xlo, xhi = refs[:9]
    gowns, lines = refs[9 : 9 + parts], refs[9 + parts : 9 + 2 * parts]
    grad_ref, force_ref = refs[9 + 2 * parts :]
    lane = lax.broadcasted_iota(jnp.int32, (1, SLOTS), 1)
    for c in range(CELLS):
        x, y, z = (at + 1 for at in own_xyz(c))
        feat, line = gathered(x, y, z, rest_ref, rlines_ref, (zlo, zhi), (ylo, yhi), (xlo, xhi))
        for gown, own_line in zip(gowns, lines):
            feat = feat + gown[c * SLOTS : (c + 1) * SLOTS, :]
            line = line + own_line[c : c + 1, :]
        grad_ref[c] = feat
        for k in range(3):
            x, y, z = own_xyz(c)
            force = jnp.where(lane < counts_ref[x, y, z], -line[:, k * SLOTS : (k + 1) * SLOTS], 0.0)
            force_ref[x, y, k, z : z + 1, :] = force


VMEM_SPEC = pl.BlockSpec(memory_space=pltpu.VMEM)
SMEM_SPEC = pl.BlockSpec(memory_space=pltpu.SMEM)


def call(kernel, name, shapes, args, scalars=0, scratch=(), limit=16, flops=0):
    out_shape = tuple(jax.ShapeDtypeStruct(shape, dtype) for shape, dtype in shapes)
    return pl.pallas_call(
        kernel,
        out_shape=out_shape,
        in_specs=[SMEM_SPEC] * scalars + [VMEM_SPEC] * (len(args) - scalars),
        out_specs=tuple(VMEM_SPEC for _ in shapes),
        scratch_shapes=list(scratch),
        compiler_params=pltpu.CompilerParams(vmem_limit_bytes=limit * 1024 * 1024),
        cost_estimate=pl.CostEstimate(flops=flops, bytes_accessed=1 << 20, transcendentals=0),
        name=name,
    )(*args)


def faces(cells):
    return [((cells, ROW, K), BF16)] * 2


def own_forward(own, rw, first, count):
    return call(
        partial(own_forward_kernel, first),
        "own_forward",
        [((count, NM, SLOTS, K), F32)],
        (own, rw),
        scratch=[
            pltpu.VMEM((OWN, K), BF16),
            pltpu.VMEM((8, OWN), F32),
            pltpu.VMEM((3, OWN, 128), F32),
            pltpu.VMEM((ROWS, OWN), BF16),
            pltpu.VMEM((ROWS, K), F32),
        ],
        flops=8 * count * ROWS * OWN * K,
    )[0]


def own_backward(own, rw, cot, first, count):
    return call(
        partial(own_backward_kernel, first, count),
        "own_backward",
        [((OWN, K), F32), ((CELLS, 128), F32)],
        (own, rw, cot),
        scratch=[
            pltpu.VMEM((OWN, K), BF16),
            pltpu.VMEM((8, OWN), F32),
            pltpu.VMEM((3, OWN, 128), F32),
            pltpu.VMEM((ROWS, OWN), BF16),
            pltpu.VMEM((ROWS, K), BF16),
            pltpu.VMEM((1, ROWS, 256), F32),
            pltpu.VMEM((8, OWN), F32),
            pltpu.VMEM((128, 128), F32),
            pltpu.VMEM((K, OWN), F32),
        ],
        flops=16 * count * ROWS * OWN * K,
    )


def ghost(counts, edges, payloads, moms, species, rw, mix, skip, readout):
    return call(
        partial(ghost_kernel, len(moms)),
        "ghost",
        [((OWN, K), BF16)]
        + faces(16)
        + [((32, SLOTS, K), F32), ((32, 128), F32), ((CELLS, NM, SLOTS, K), F32)],
        (counts, edges, *payloads, *moms, species, rw, mix, skip, readout),
        scalars=2,
        scratch=[
            pltpu.VMEM((64, SLOTS, K), BF16),
            pltpu.VMEM((3, 64, 128), F32),
            pltpu.VMEM((64, 128), F32),
            pltpu.VMEM((GWIDTH, K), BF16),
            pltpu.VMEM((8, GWIDTH), F32),
            pltpu.VMEM((OWN, K), BF16),
            pltpu.VMEM((8, OWN), F32),
            pltpu.VMEM((3, OWN, 128), F32),
            pltpu.VMEM((OWN, 128), F32),
            pltpu.VMEM((CELLS, ROWS, GWIDTH), BF16),
            pltpu.VMEM((ROWS, K), F32),
            pltpu.VMEM((CELLS, NM, SLOTS, K), F32),
            pltpu.VMEM((ROWS, K), BF16),
            pltpu.VMEM((2, ROWS, 256), F32),
            pltpu.VMEM((8, GWIDTH), F32),
            pltpu.VMEM((128, 128), F32),
            pltpu.VMEM((64, SLOTS, K), F32),
            pltpu.VMEM((3, 64, 128), F32),
            pltpu.VMEM((8, OWN), F32),
            pltpu.VMEM((CELLS, 128), F32),
        ],
        limit=40,
        flops=16 * CELLS * ROWS * GWIDTH * K,
    )


def moved(lo, hi, axis, ring):
    size = lax.axis_size(axis)
    up = [(i, (i + 1) % size) for i in range(size if ring else size - 1)]
    down = [(j, i) for i, j in up]
    return lax.ppermute(hi, axis, up), lax.ppermute(lo, axis, down)


FORWARD_PARTS = ((0, 2), (2, 2), (4, 4))
BACKWARD_PARTS = ((0, 4), (4, 2), (6, 2))


def after(values, done):
    return lax.optimization_barrier((values, done))[0]


def shards(features, positions, counts, species, radial_weight, mix_weight, skip_weight, readout):
    plane = lax.axis_index("gz")
    edges = jnp.stack([plane == 0, plane == lax.axis_size("gz") - 1]).astype(jnp.int32)
    rw = jnp.transpose(radial_weight, (1, 0, 2))
    own, xlo, xhi = call(
        pack_x_kernel,
        "pack_x",
        [((CELLS, ROW, K), BF16)] + faces(4),
        (counts, features.reshape(CELLS, SLOTS, K), jnp.transpose(positions, (0, 1, 3, 2, 4))),
        scalars=1,
        scratch=[pltpu.VMEM((CELLS, 128), F32)],
    )
    xs = moved(xlo, xhi, "gx", True)
    moms = [own_forward(own, rw, *FORWARD_PARTS[0])]
    xs = after(xs, moms[0])
    ylo, yhi = call(pack_y_kernel, "pack_y", faces(8), (own, *xs))
    ys = moved(ylo, yhi, "gy", True)
    moms.append(own_forward(after(own, ylo), rw, *FORWARD_PARTS[1]))
    ys = after(ys, moms[1])
    zlo, zhi = call(pack_z_kernel, "pack_z", faces(16), (own, *xs, *ys))
    zs = moved(zlo, zhi, "gz", False)
    moms.append(own_forward(after(own, zlo), rw, *FORWARD_PARTS[2]))
    new, bzlo, bzhi, rest, rlines, cot = ghost(
        counts,
        edges,
        (own, *xs, *ys, *zs),
        moms,
        species.reshape(CELLS, SLOTS),
        rw,
        mix_weight,
        skip_weight,
        readout,
    )
    zs = moved(bzlo, bzhi, "gz", False)
    backs = [own_backward(own, rw, cot, *BACKWARD_PARTS[0])]
    zs = after(zs, backs[0][0])
    bylo, byhi = call(back_y_kernel, "back_y", faces(8), (rest, rlines, *zs))
    ys = moved(bylo, byhi, "gy", True)
    backs.append(own_backward(after(own, bylo), rw, cot, *BACKWARD_PARTS[1]))
    ys = after(ys, backs[1][0])
    bxlo, bxhi = call(back_x_kernel, "back_x", faces(4), (rest, rlines, *zs, *ys))
    xs = moved(bxlo, bxhi, "gx", True)
    backs.append(own_backward(after(own, bxlo), rw, cot, *BACKWARD_PARTS[2]))
    grad, force = call(
        partial(finish_kernel, len(backs)),
        "finish",
        [((CELLS, SLOTS, K), F32), ((2, 2, 3, 2, SLOTS), F32)],
        (counts, rest, rlines, *zs, *ys, *xs, *(b[0] for b in backs), *(b[1] for b in backs)),
        scalars=1,
    )
    return (
        new.reshape(2, 2, 2, SLOTS, K),
        jnp.transpose(force, (0, 1, 3, 2, 4)),
        grad.reshape(2, 2, 2, SLOTS, K),
    )


def solution(mesh):
    cells = P("gx", "gy", "gz", None, None)
    return jax.shard_map(
        shards,
        mesh=mesh,
        in_specs=(cells, cells, P("gx", "gy", "gz"), P("gx", "gy", "gz", None), P(), P(), P(), P()),
        out_specs=(cells, cells, cells),
        check_vma=False,
    )
```

time: 635 us -> 97.8 us (0.15); the launches traced: 628 us -> 97.5 us
  local copies, waits for them, and re-layouts: 213 us -> 2.96 us
  other arithmetic: 210 us -> 0.08 us
  matrix products: 97.5 us -> 0 us
  Pallas kernels: 0 us -> 52.9 us
  loops' own time: 44.1 us -> 0 us
  starting transfers between devices: 39.3 us -> 28.4 us
  waiting for transfers between devices: 23 us -> 12.3 us
    dot_general x128 -> x0, matrix products: 97.5 us -> none  [the longest x24 70.3 us: cell_terms(): jnp.dot(table, near_feat, preferred_element_type=jnp.float32)]
    reduce_sum x64 -> x0, other arithmetic: 75.5 us -> none  [the longest x8 38.5 us: pair_table(): table = radial[:, None] * harmonics(unit)[None]]
    mul x57 -> x0, other arithmetic: 65.5 us -> none  [the longest x16 49.5 us: pair_table(): math.sqrt(2.0 / CUTOFF) * jnp.sin(freqs[:, None, None] * scaled[None])]
    dynamic_update_slice x64 -> x0, local copies, waits for them, and re-layouts: 63.7 us -> none  [total(): energies, updated = lax.map(per_cell, (grid, kinds_flat, alive_flat))]
    reshape x16 -> x0, local copies, waits for them, and re-layouts: 56 us -> none  [the longest x8 55.2 us: pair_table(): return table.reshape(nbasis * 9 * slots, width).astype(jnp.bfloat16)]
    pallas_call x0 -> x13, Pallas kernels: none -> 52.9 us  [call(): pl.pallas_call(kernel, out_shape=out_shape, in_specs=[SMEM_SPEC] * scalar...]
    another operation x2 -> x0, loops' own time: 44.1 us -> none  [total(): energies, updated = lax.map(per_cell, (grid, kinds_flat, alive_flat))]
    dynamic_slice x56 -> x0, local copies, waits for them, and re-layouts: 30.5 us -> none  [the longest x48 30.3 us: total(): energies, updated = lax.map(per_cell, (grid, kinds_flat, alive_flat))]
  transfers between devices with their start and end apart: 24 -> 12, of which waited for: 12 -> 4; matrix products, arithmetic and copies ran while one was open for 1% -> 0% of each run, Pallas kernels for 0% -> 17%
where the time goes in v1:
time: 97.8 us; the launch traced here: 97.5 us
  Pallas kernels  52.9 us (54%)
  starting transfers between devices  28.4 us (29%)
  waiting for transfers between devices  12.3 us (13%)
  local copies, waits for them, and re-layouts  2.96 us (3%)
    pallas_call x13, Pallas kernels, call(): pl.pallas_call(kernel, out_shape=out_shape, in_specs=[SMEM_SPEC] * scalar...  52.9 us
    ppermute x12, starting transfers between devices, moved(): return (lax.ppermute(hi, axis, up), lax.ppermute(lo, axis, down))  28.4 us
    ppermute x12, waiting for transfers between devices, moved(): return (lax.ppermute(hi, axis, up), lax.ppermute(lo, axis, down))  12.3 us
    unnamed x20, local copies, waits for them, and re-layouts  2.96 us
  transfers between devices with their start and end apart: 12, of which 4 were waited for; matrix products, arithmetic and copies ran while one was open for 0% of the time, Pallas kernels for 17%

profile of v1, /device:TPU:8, one launch (start us, length us, event | category | flops | bytes accessed | tf_op | source)
XLA Modules:
  0.0 97.5 jit_solution(6236407732896081758)
XLA Ops:
  0.6 0.8 copy-done
  1.5 0.7 copy-done.1
  2.2 0.7 copy-done.2
  2.9 0.7 pack_x.1
  3.5 2.0 %collective-permute-start = (bf16[4,48,128]{2,1,0:T(8,128)(2,1)S(1)}, bf16[4,48,128]{2,1,0:T(8,128)(2,1)S(1)}, u32[]{:S(2)}, u32[]{:S(2)}) collective-permute-start(bf16[4,48,128]{2,1,0:T(8,128)(2,1)S(1)} %get-tuple-element.41), channel_id=1, source_target_pairs={{0,16},{16,32},{32,48},{48,64},{64,80},{80,96},{96,112},{112,128},... | collective-permute-start | bytes 147464 | tf_op jit(solution)/shard_map/ppermute | solution.py:645
  5.5 5.8 %collective-permute-start.1 = (bf16[4,48,128]{2,1,0:T(8,128)(2,1)S(1)}, bf16[4,48,128]{2,1,0:T(8,128)(2,1)S(1)}, u32[]{:S(2)}, u32[]{:S(2)}) collective-permute-start(bf16[4,48,128]{2,1,0:T(8,128)(2,1)S(1)} %get-tuple-element.42), channel_id=1, source_target_pairs={{16,0},{32,16},{48,32},{64,48},{80,64},{96,80},{112,96},{128,112},... | collective-permute-start | bytes 147464 | tf_op jit(solution)/shard_map/ppermute | solution.py:645
  11.3 0.7 copy-done.6
  12.0 1.4 %own_forward.3.refs_9_ = f32[2,9,32,128]{3,2,1,0:T(8,128)S(1)} custom-call(bf16[8,48,128]{2,1,0:T(8,128)(2,1)S(1)} %get-tuple-element.70.own_ref.own.refs_2_, f32[3,8,128]{2,1,0:T(8,128)S(1)} %bitcast.11), custom_call_target="tpu_custom_call" | custom-call | flops 1207959552 | bytes 1048576 | tf_op jit(solution)/shard_map/own_forward/pallas_call | solution.py:551
  13.4 0.1 add_convert_fusion.refs_1_
  13.5 2.8 %collective-permute-start.3 = (bf16[8,48,128]{2,1,0:T(8,128)(2,1)S(1)}, bf16[8,48,128]{2,1,0:T(8,128)(2,1)S(1)}, u32[]{:S(2)}, u32[]{:S(2)}) collective-permute-start(bf16[8,48,128]{2,1,0:T(8,128)(2,1)S(1)} %get-tuple-element.46), channel_id=1, source_target_pairs={{4,0},{8,4},{12,8},{0,12},{5,1},{9,5},{13,9},{1,13},{6,2},{10,6},{... | collective-permute-start | bytes 294920 | tf_op jit(solution)/shard_map/ppermute | solution.py:645
  16.4 1.4 %own_forward.4.refs_10_ = f32[2,9,32,128]{3,2,1,0:T(8,128)S(1)} custom-call(bf16[8,48,128]{2,1,0:T(8,128)(2,1)S(1)} %get-tuple-element.70.own_ref.own.refs_2_, f32[3,8,128]{2,1,0:T(8,128)S(1)} %bitcast.12), custom_call_target="tpu_custom_call" | custom-call | flops 1207959552 | bytes 1048576 | tf_op jit(solution)/shard_map/own_forward/pallas_call | solution.py:551
  17.8 4.4 %collective-permute-done.2.ylo.refs_5_ = bf16[8,48,128]{2,1,0:T(8,128)(2,1)S(1)} collective-permute-done((bf16[8,48,128]{2,1,0:T(8,128)(2,1)S(1)}, bf16[8,48,128]{2,1,0:T(8,128)(2,1)S(1)}, u32[]{:S(2)}, u32[]{:S(2)}) %collective-permute-start.2) | collective-permute-done | bytes 98336 | tf_op jit(solution)/shard_map/ppermute | solution.py:645
  22.2 1.9 %collective-permute-start.5 = (bf16[16,48,128]{2,1,0:T(8,128)(2,1)S(1)}, bf16[16,48,128]{2,1,0:T(8,128)(2,1)S(1)}, u32[]{:S(2)}, u32[]{:S(2)}) collective-permute-start(bf16[16,48,128]{2,1,0:T(8,128)(2,1)S(1)} %get-tuple-element.51), channel_id=1, source_target_pairs={{1,0},{2,1},{3,2},{5,4},{6,5},{7,6},{9,8},{10,9},{11,10},{13,12},{... | collective-permute-start | bytes 589832 | tf_op jit(solution)/shard_map/ppermute | solution.py:645
  24.2 0.0 copy-start.3
  24.2 0.0 copy-start.8
  24.2 2.5 %collective-permute-start.4 = (bf16[16,48,128]{2,1,0:T(8,128)(2,1)S(1)}, bf16[16,48,128]{2,1,0:T(8,128)(2,1)S(1)}, u32[]{:S(2)}, u32[]{:S(2)}) collective-permute-start(bf16[16,48,128]{2,1,0:T(8,128)(2,1)S(1)} %get-tuple-element.50), channel_id=1, source_target_pairs={{0,1},{1,2},{2,3},{4,5},{5,6},{6,7},{8,9},{9,10},{10,11},{12,13},{... | collective-permute-start | bytes 589832 | tf_op jit(solution)/shard_map/ppermute | solution.py:645
  26.8 2.6 %own_forward.5.refs_11_ = f32[4,9,32,128]{3,2,1,0:T(8,128)S(1)} custom-call(bf16[8,48,128]{2,1,0:T(8,128)(2,1)S(1)} %get-tuple-element.70.own_ref.own.refs_2_, f32[3,8,128]{2,1,0:T(8,128)S(1)} %bitcast.13), custom_call_target="tpu_custom_call" | custom-call | flops 2415919104 | bytes 1048576 | tf_op jit(solution)/shard_map/own_forward/pallas_call | solution.py:551
  29.4 2.0 %collective-permute-done.4.refs_7_ = bf16[16,48,128]{2,1,0:T(8,128)(2,1)S(1)} collective-permute-done((bf16[16,48,128]{2,1,0:T(8,128)(2,1)S(1)}, bf16[16,48,128]{2,1,0:T(8,128)(2,1)S(1)}, u32[]{:S(2)}, u32[]{:S(2)}) %collective-permute-start.4) | collective-permute-done | bytes 196640 | tf_op jit(solution)/shard_map/ppermute | solution.py:645
  31.4 34.3 %ghost.1 = (bf16[256,128]{1,0:T(8,128)(2,1)}, bf16[16,48,128]{2,1,0:T(8,128)(2,1)S(1)}, bf16[16,48,128]{2,1,0:T(8,128)(2,1)S(1)}, f32[32,32,128]{2,1,0:T(8,128)S...) custom-call(s32[2,2,2]{2,1,0:T(2,128)S(1)} %copy-done.3, s32[2]{0:T(128)S(1)} %add_convert_fusion.refs_1_, ...), custom_call_target="tpu_custom_call" | custom-call | flops 24159191040 | bytes 1048576 | tf_op jit(solution)/shard_map/ghost/pallas_call | solution.py:551
  65.7 1.9 %collective-permute-start.6 = (bf16[16,48,128]{2,1,0:T(8,128)(2,1)S(1)}, bf16[16,48,128]{2,1,0:T(8,128)(2,1)S(1)}, u32[]{:S(2)}, u32[]{:S(2)}) collective-permute-start(bf16[16,48,128]{2,1,0:T(8,128)(2,1)S(1)} %get-tuple-element.56), channel_id=1, source_target_pairs={{0,1},{1,2},{2,3},{4,5},{5,6},{6,7},{8,9},{9,10},{10,11},{12,13},{... | collective-permute-start | bytes 589832 | tf_op jit(solution)/shard_map/ppermute | solution.py:645
  67.6 3.6 %collective-permute-start.7 = (bf16[16,48,128]{2,1,0:T(8,128)(2,1)S(1)}, bf16[16,48,128]{2,1,0:T(8,128)(2,1)S(1)}, u32[]{:S(2)}, u32[]{:S(2)}) collective-permute-start(bf16[16,48,128]{2,1,0:T(8,128)(2,1)S(1)} %get-tuple-element.57), channel_id=1, source_target_pairs={{1,0},{2,1},{3,2},{5,4},{6,5},{7,6},{9,8},{10,9},{11,10},{13,12},{... | collective-permute-start | bytes 589832 | tf_op jit(solution)/shard_map/ppermute | solution.py:645
  71.2 5.4 %own_backward.3 = (f32[256,128]{1,0:T(8,128)S(1)}, f32[8,128]{1,0:T(8,128)S(1)}) custom-call(bf16[8,48,128]{2,1,0:T(8,128)(2,1)S(1)} %get-tuple-element.70.own_ref.own.refs_2_, f32[3,8,128]{2,1,0:T(8,128)S(1)} %bitcast.15, f32[8,9,32,128]{3,2,1,0:T(8,128)S(1)} %get-tuple-element.58.mom_ref), custom_call_target="tpu_custom_call" | custom-call | flops 4831838208 | bytes 1048576 | tf_op jit(solution)/shard_map/own_backward/pallas_call | solution.py:551
  76.6 0.1 back_y.1
  76.7 0.3 collective-permute-start.9
  76.9 2.0 %collective-permute-start.8 = (bf16[8,48,128]{2,1,0:T(8,128)(2,1)S(1)}, bf16[8,48,128]{2,1,0:T(8,128)(2,1)S(1)}, u32[]{:S(2)}, u32[]{:S(2)}) collective-permute-start(bf16[8,48,128]{2,1,0:T(8,128)(2,1)S(1)} %get-tuple-element.62), channel_id=1, source_target_pairs={{0,4},{4,8},{8,12},{12,0},{1,5},{5,9},{9,13},{13,1},{2,6},{6,10},{... | collective-permute-start | bytes 294920 | tf_op jit(solution)/shard_map/ppermute | solution.py:645
  79.0 2.8 %own_backward.4 = (f32[256,128]{1,0:T(8,128)S(1)}, f32[8,128]{1,0:T(8,128)S(1)}) custom-call(bf16[8,48,128]{2,1,0:T(8,128)(2,1)S(1)} %get-tuple-element.70.own_ref.own.refs_2_, f32[3,8,128]{2,1,0:T(8,128)S(1)} %bitcast.16, f32[8,9,32,128]{3,2,1,0:T(8,128)S(1)} %get-tuple-element.58.mom_ref), custom_call_target="tpu_custom_call" | custom-call | flops 2415919104 | bytes 1048576 | tf_op jit(solution)/shard_map/own_backward/pallas_call | solution.py:551
  81.8 1.0 %collective-permute-done.8.ylo.refs_5_ = bf16[8,48,128]{2,1,0:T(8,128)(2,1)S(1)} collective-permute-done((bf16[8,48,128]{2,1,0:T(8,128)(2,1)S(1)}, bf16[8,48,128]{2,1,0:T(8,128)(2,1)S(1)}, u32[]{:S(2)}, u32[]{:S(2)}) %collective-permute-start.8) | collective-permute-done | bytes 98336 | tf_op jit(solution)/shard_map/ppermute | solution.py:645
  82.9 0.1 back_x.1
  82.9 5.6 %collective-permute-start.11 = (bf16[4,48,128]{2,1,0:T(8,128)(2,1)S(1)}, bf16[4,48,128]{2,1,0:T(8,128)(2,1)S(1)}, u32[]{:S(2)}, u32[]{:S(2)}) collective-permute-start(bf16[4,48,128]{2,1,0:T(8,128)(2,1)S(1)} %get-tuple-element.69), channel_id=1, source_target_pairs={{16,0},{32,16},{48,32},{64,48},{80,64},{96,80},{112,96},{128,112},... | collective-permute-start | bytes 147464 | tf_op jit(solution)/shard_map/ppermute | solution.py:645
  88.5 2.9 %own_backward.5 = (f32[256,128]{1,0:T(8,128)S(1)}, f32[8,128]{1,0:T(8,128)S(1)}) custom-call(bf16[8,48,128]{2,1,0:T(8,128)(2,1)S(1)} %get-tuple-element.70.own_ref.own.refs_2_, f32[3,8,128]{2,1,0:T(8,128)S(1)} %bitcast.17, f32[8,9,32,128]{3,2,1,0:T(8,128)S(1)} %get-tuple-element.58.mom_ref), custom_call_target="tpu_custom_call" | custom-call | flops 2415919104 | bytes 1048576 | tf_op jit(solution)/shard_map/own_backward/pallas_call | solution.py:551
  91.3 4.8 %collective-permute-done.10.refs_7_ = bf16[4,48,128]{2,1,0:T(8,128)(2,1)S(1)} collective-permute-done((bf16[4,48,128]{2,1,0:T(8,128)(2,1)S(1)}, bf16[4,48,128]{2,1,0:T(8,128)(2,1)S(1)}, u32[]{:S(2)}, u32[]{:S(2)}) %collective-permute-start.10) | collective-permute-done | bytes 49184 | tf_op jit(solution)/shard_map/ppermute | solution.py:645
  96.2 1.3 %finish.1 = (f32[8,32,128]{2,1,0:T(8,128)}, f32[2,2,3,2,32]{4,3,2,1,0:T(2,128)}) custom-call(s32[2,2,2]{2,1,0:T(2,128)S(1)} %copy-done.3, f32[32,32,128]{2,1,0:T(8,128)S(1)} %get-tuple-element.54.rest_ref.refs_1_, f32[32,128]{1,0:T(8,128)S(1)} %get-tuple-element.55.rlines_ref.refs_2_, bf16[16,48,128]{2,1,0:T(8,128)(2,1)S(1)} %collective-permute-done.6.zlo.refs_3_, ...), custom_call_target="tpu_custom_call" | custom-call | bytes 1048576 | tf_op jit(solution)/shard_map/finish/pallas_call | solution.py:551
  (26 shorter events, 0.1 us)
Async XLA Ops:
  0.6 0.8 copy-start
  1.5 0.7 copy-start.1
  2.2 0.7 copy-start.2
  3.5 10.0 %collective-permute-start = (bf16[4,48,128]{2,1,0:T(8,128)(2,1)S(1)}, bf16[4,48,128]{2,1,0:T(8,128)(2,1)S(1)}, u32[]{:S(2)}, u32[]{:S(2)}) collective-permute-start(bf16[4,48,128]{2,1,0:T(8,128)(2,1)S(1)} %get-tuple-element.41), channel_id=1, source_target_pairs={{0,16},{16,32},{32,48},{48,64},{64,80},{80,96},{96,112},{112,128},... | collective-permute-start | bytes 147464 | tf_op jit(solution)/shard_map/ppermute | solution.py:645
  5.5 8.0 %collective-permute-start.1 = (bf16[4,48,128]{2,1,0:T(8,128)(2,1)S(1)}, bf16[4,48,128]{2,1,0:T(8,128)(2,1)S(1)}, u32[]{:S(2)}, u32[]{:S(2)}) collective-permute-start(bf16[4,48,128]{2,1,0:T(8,128)(2,1)S(1)} %get-tuple-element.42), channel_id=1, source_target_pairs={{16,0},{32,16},{48,32},{64,48},{80,64},{96,80},{112,96},{128,112},... | collective-permute-start | bytes 147464 | tf_op jit(solution)/shard_map/ppermute | solution.py:645
  11.3 0.7 copy-start.6
  12.0 4.4 %copy-start.7 = (f32[8,3,128]{2,0,1:T(8,128)S(1)}, f32[8,3,128]{2,0,1:T(8,128)}, u32[]{:S(2)}) copy-start(f32[8,3,128]{2,0,1:T(8,128)} %param.12) | copy-start | bytes 36868
  13.5 8.7 %collective-permute-start.3 = (bf16[8,48,128]{2,1,0:T(8,128)(2,1)S(1)}, bf16[8,48,128]{2,1,0:T(8,128)(2,1)S(1)}, u32[]{:S(2)}, u32[]{:S(2)}) collective-permute-start(bf16[8,48,128]{2,1,0:T(8,128)(2,1)S(1)} %get-tuple-element.46), channel_id=1, source_target_pairs={{4,0},{8,4},{12,8},{0,12},{5,1},{9,5},{13,9},{1,13},{6,2},{10,6},{... | collective-permute-start | bytes 294920 | tf_op jit(solution)/shard_map/ppermute | solution.py:645
  16.4 5.8 %collective-permute-start.2 = (bf16[8,48,128]{2,1,0:T(8,128)(2,1)S(1)}, bf16[8,48,128]{2,1,0:T(8,128)(2,1)S(1)}, u32[]{:S(2)}, u32[]{:S(2)}) collective-permute-start(bf16[8,48,128]{2,1,0:T(8,128)(2,1)S(1)} %get-tuple-element.45), channel_id=1, source_target_pairs={{0,4},{4,8},{8,12},{12,0},{1,5},{5,9},{9,13},{13,1},{2,6},{6,10},{... | collective-permute-start | bytes 294920 | tf_op jit(solution)/shard_map/ppermute | solution.py:645
  22.2 9.1 %collective-permute-start.5 = (bf16[16,48,128]{2,1,0:T(8,128)(2,1)S(1)}, bf16[16,48,128]{2,1,0:T(8,128)(2,1)S(1)}, u32[]{:S(2)}, u32[]{:S(2)}) collective-permute-start(bf16[16,48,128]{2,1,0:T(8,128)(2,1)S(1)} %get-tuple-element.51), channel_id=1, source_target_pairs={{1,0},{2,1},{3,2},{5,4},{6,5},{7,6},{9,8},{10,9},{11,10},{13,12},{... | collective-permute-start | bytes 589832 | tf_op jit(solution)/shard_map/ppermute | solution.py:645
  24.2 7.2 %copy-start.3 = (s32[2,2,2]{2,1,0:T(2,128)S(1)}, s32[2,2,2]{2,1,0:T(2,128)}, u32[]{:S(2)}) copy-start(s32[2,2,2]{2,1,0:T(2,128)} %refs_0_.3) | copy-start | bytes 100
  24.2 7.2 %copy-start.4 = (bf16[5,128,128]{2,1,0:T(8,128)(2,1)S(1)}, bf16[5,128,128]{2,1,0:T(8,128)(2,1)}, u32[]{:S(2)}) copy-start(bf16[5,128,128]{2,1,0:T(8,128)(2,1)} %refs_15_.1) | copy-start | bytes 491524
  24.2 7.2 %copy-start.5 = (bf16[128,128]{1,0:T(8,128)(2,1)S(1)}, bf16[128,128]{1,0:T(8,128)(2,1)}, u32[]{:S(2)}) copy-start(bf16[128,128]{1,0:T(8,128)(2,1)} %refs_14_.1) | copy-start | bytes 98308
  24.2 7.2 %copy-start.8 = (s32[2,2,2,32]{3,2,1,0:T(2,128)S(1)}, s32[2,2,2,32]{3,2,1,0:T(2,128)}, u32[]{:S(2)}) copy-start(s32[2,2,2,32]{3,2,1,0:T(2,128)} %param.11) | copy-start | bytes 3076
  24.2 7.2 %copy-start.9 = (f32[5,128]{1,0:T(8,128)S(1)}, f32[5,128]{1,0:T(8,128)}, u32[]{:S(2)}) copy-start(f32[5,128]{1,0:T(8,128)} %refs_16_.1) | copy-start | bytes 7684
  24.2 7.1 %collective-permute-start.4 = (bf16[16,48,128]{2,1,0:T(8,128)(2,1)S(1)}, bf16[16,48,128]{2,1,0:T(8,128)(2,1)S(1)}, u32[]{:S(2)}, u32[]{:S(2)}) collective-permute-start(bf16[16,48,128]{2,1,0:T(8,128)(2,1)S(1)} %get-tuple-element.50), channel_id=1, source_target_pairs={{0,1},{1,2},{2,3},{4,5},{5,6},{6,7},{8,9},{9,10},{10,11},{12,13},{... | collective-permute-start | bytes 589832 | tf_op jit(solution)/shard_map/ppermute | solution.py:645
  65.7 10.9 %collective-permute-start.6 = (bf16[16,48,128]{2,1,0:T(8,128)(2,1)S(1)}, bf16[16,48,128]{2,1,0:T(8,128)(2,1)S(1)}, u32[]{:S(2)}, u32[]{:S(2)}) collective-permute-start(bf16[16,48,128]{2,1,0:T(8,128)(2,1)S(1)} %get-tuple-element.56), channel_id=1, source_target_pairs={{0,1},{1,2},{2,3},{4,5},{5,6},{6,7},{8,9},{9,10},{10,11},{12,13},{... | collective-permute-start | bytes 589832 | tf_op jit(solution)/shard_map/ppermute | solution.py:645
  67.6 9.0 %collective-permute-start.7 = (bf16[16,48,128]{2,1,0:T(8,128)(2,1)S(1)}, bf16[16,48,128]{2,1,0:T(8,128)(2,1)S(1)}, u32[]{:S(2)}, u32[]{:S(2)}) collective-permute-start(bf16[16,48,128]{2,1,0:T(8,128)(2,1)S(1)} %get-tuple-element.57), channel_id=1, source_target_pairs={{1,0},{2,1},{3,2},{5,4},{6,5},{7,6},{9,8},{10,9},{11,10},{13,12},{... | collective-permute-start | bytes 589832 | tf_op jit(solution)/shard_map/ppermute | solution.py:645
  76.7 6.2 %collective-permute-start.9 = (bf16[8,48,128]{2,1,0:T(8,128)(2,1)S(1)}, bf16[8,48,128]{2,1,0:T(8,128)(2,1)S(1)}, u32[]{:S(2)}, u32[]{:S(2)}) collective-permute-start(bf16[8,48,128]{2,1,0:T(8,128)(2,1)S(1)} %get-tuple-element.63), channel_id=1, source_target_pairs={{4,0},{8,4},{12,8},{0,12},{5,1},{9,5},{13,9},{1,13},{6,2},{10,6},{... | collective-permute-start | bytes 294920 | tf_op jit(solution)/shard_map/ppermute | solution.py:645
  76.9 5.9 %collective-permute-start.8 = (bf16[8,48,128]{2,1,0:T(8,128)(2,1)S(1)}, bf16[8,48,128]{2,1,0:T(8,128)(2,1)S(1)}, u32[]{:S(2)}, u32[]{:S(2)}) collective-permute-start(bf16[8,48,128]{2,1,0:T(8,128)(2,1)S(1)} %get-tuple-element.62), channel_id=1, source_target_pairs={{0,4},{4,8},{8,12},{12,0},{1,5},{5,9},{9,13},{13,1},{2,6},{6,10},{... | collective-permute-start | bytes 294920 | tf_op jit(solution)/shard_map/ppermute | solution.py:645
  82.9 13.3 %collective-permute-start.11 = (bf16[4,48,128]{2,1,0:T(8,128)(2,1)S(1)}, bf16[4,48,128]{2,1,0:T(8,128)(2,1)S(1)}, u32[]{:S(2)}, u32[]{:S(2)}) collective-permute-start(bf16[4,48,128]{2,1,0:T(8,128)(2,1)S(1)} %get-tuple-element.69), channel_id=1, source_target_pairs={{16,0},{32,16},{48,32},{64,48},{80,64},{96,80},{112,96},{128,112},... | collective-permute-start | bytes 147464 | tf_op jit(solution)/shard_map/ppermute | solution.py:645
  88.5 7.7 %collective-permute-start.10 = (bf16[4,48,128]{2,1,0:T(8,128)(2,1)S(1)}, bf16[4,48,128]{2,1,0:T(8,128)(2,1)S(1)}, u32[]{:S(2)}, u32[]{:S(2)}) collective-permute-start(bf16[4,48,128]{2,1,0:T(8,128)(2,1)S(1)} %get-tuple-element.68), channel_id=1, source_target_pairs={{0,16},{16,32},{32,48},{48,64},{64,80},{80,96},{96,112},{112,128},... | collective-permute-start | bytes 147464 | tf_op jit(solution)/shard_map/ppermute | solution.py:645

commit v2 on v1

--- a/solution.py
+++ b/solution.py
@@ -154,7 +154,7 @@
         for k in range(3):
             x, y, z = own_xyz(c)
             value = pos_ref[x, y, k, z : z + 1, :]
-            value = jnp.where(lane < counts_ref[x, y, z], value, SENTINEL)
+            value = jnp.where(lane < counts_ref[x, y : y + 1, z : z + 1], value, SENTINEL)
             line_ref[c : c + 1, k * SLOTS : (k + 1) * SLOTS] = value
     pieces = split_line(line_ref[...], 3)
     for c in range(CELLS):
@@ -207,8 +207,8 @@
         lanes = slice(tile * 128, tile * 128 + 128)
         for block in range(2):
             inv, ux, uy, uz, first, cosine, env, denv = geometry(block, tile)
-            radial = [value * env for value in sine_series(first, cosine)]
-            shape = harmonics(ux, uy, uz)
+            radial = [(value * env).astype(BF16) for value in sine_series(first, cosine)]
+            shape = [None] + [value.astype(BF16) for value in harmonics(ux, uy, uz)[1:]]
             for b in range(NB):
                 for m in range(NM):
                     row = block * HALF + (b * NM + m) * 16
@@ -234,6 +234,12 @@
                 row = block * HALF + (b * NM + m) * 16
                 weight = rw_ref[DEG[m], b : b + 1, :]
                 dd_ref[row : row + 16, :] = (cot * weight).astype(BF16)
+
+
+def pairwise(terms):
+    while len(terms) > 2:
+        terms = [a + b for a, b in zip(terms[::2], terms[1::2])]
+    return terms[0].astype(F32) + terms[1].astype(F32)
 
 
 def pair_forces(geometry, dd_ref, nf_ref, dt_ref, width, near_out, fown_ref):
@@ -248,21 +254,20 @@
             near_sum = [None] * 3
             for block in range(2):
                 inv, ux, uy, uz, first, cosine, env, denv = geometry(block, tile)
-                sines = sine_series(first, cosine)
-                cosines = cosine_series(cosine)
+                sines = [v.astype(BF16) for v in sine_series(first, cosine)]
+                cosines = [v.astype(BF16) for v in cosine_series(cosine)]
                 shape = harmonics(ux, uy, uz)
                 pull = [None] * NM
                 total_s = None
                 total_c = None
                 for m in range(NM):
-                    part_s = None
-                    part_c = None
+                    ones, twos = [], []
                     for b in range(NB):
                         row = block * HALF + (b * NM + m) * 16
-                        value = slab[row : row + 16, inside]
-                        one, two = value * sines[b], value * cosines[b]
-                        part_s = one if part_s is None else part_s + one
-                        part_c = two if part_c is None else part_c + two
+                        value = slab[row : row + 16, inside].astype(BF16)
+                        ones.append(value * sines[b])
+                        twos.append(value * cosines[b])
+                    part_s, part_c = pairwise(ones), pairwise(twos)
                     pull[m] = part_s
                     if m == 0:
                         total_s, total_c = part_s, part_c
@@ -295,16 +300,25 @@
 def own_forward_kernel(first, own_ref, rw_ref, mom_ref, nf_ref, near_ref, ownpos_ref, table_ref, dens_ref):
     load_own(own_ref, nf_ref, near_ref, ownpos_ref)
 
-    def step(at, carry):
-        cell = first + at
-        build_table(table_ref, lambda b, t: geometry_of(near_ref, ownpos_ref, cell, b, t, True), 2)
-        dens_ref[...] = jnp.dot(table_ref[...], nf_ref[...], preferred_element_type=F32)
-        for block in range(2):
-            for m in range(NM):
-                mom_ref[at, m, block * 16 : block * 16 + 16, :] = weigh(dens_ref, rw_ref, block, m)
+    def step(pair, carry):
+        for side in range(2):
+            cell = first + pair * 2 + side
+
+            def geometry(block, tile, cell=cell):
+                return geometry_of(near_ref, ownpos_ref, cell, block, tile, True)
+
+            build_table(table_ref.at[side], geometry, 2)
+        for side in range(2):
+            dens_ref[side] = jnp.dot(table_ref[side], nf_ref[...], preferred_element_type=F32)
+        for side in range(2):
+            at = pair * 2 + side
+            for block in range(2):
+                for m in range(NM):
+                    rows = slice(block * 16, block * 16 + 16)
+                    mom_ref[at, m, rows, :] = weigh(dens_ref.at[side], rw_ref, block, m)
         return carry
 
-    lax.fori_loop(0, mom_ref.shape[0], step, 0)
+    lax.fori_loop(0, mom_ref.shape[0] // 2, step, 0)
 
 
 def own_backward_kernel(
@@ -321,22 +335,27 @@
         for k in range(3):
             gnear_ref[k : k + 1, tile * 128 : tile * 128 + 128] += sums[k]
 
-    def step(at, carry):
-        cell = first + at
-
-        def geometry(block, tile):
-            return geometry_of(near_ref, ownpos_ref, cell, block, tile, True)
-
-        spread(mom_ref, cell, rw_ref, dd_ref)
-        build_table(table_ref, geometry, 2)
-        gsum_ref[...] += lax.dot_general(
-            dd_ref[...], table_ref[...], (((0,), (0,)), ((), ())), preferred_element_type=F32
-        )
-        line = pair_forces(geometry, dd_ref, nf_ref, dt_ref, OWN, near_out, fown_ref)
-        lines_ref[pl.ds(cell, 1), :] = -line
+    def step(pair, carry):
+        for side in range(2):
+            cell = first + pair * 2 + side
+            spread(mom_ref, cell, rw_ref, dd_ref.at[side])
+        for side in range(2):
+            cell = first + pair * 2 + side
+
+            def geometry(block, tile, cell=cell):
+                return geometry_of(near_ref, ownpos_ref, cell, block, tile, True)
+
+            build_table(table_ref.at[side], geometry, 2)
+            gsum_ref[...] += lax.dot_general(
+                dd_ref[side], table_ref[side], (((0,), (0,)), ((), ())), preferred_element_type=F32
+            )
+            line = pair_forces(
+                geometry, dd_ref.at[side], nf_ref, dt_ref.at[side], OWN, near_out, fown_ref.at[side]
+            )
+            lines_ref[pl.ds(cell, 1), :] = -line
         return carry
 
-    lax.fori_loop(0, count, step, 0)
+    lax.fori_loop(0, count // 2, step, 0)
     gown_ref[...] = gsum_ref[...].T
     for c in range(CELLS):
         for k in range(3):
@@ -377,8 +396,8 @@
         value = jnp.where(outside, SENTINEL, lines_ref[:, k * SLOTS : (k + 1) * SLOTS])
         pos_ref[k, :, 0:SLOTS] = value + spots[k].astype(F32) * CUTOFF
     spare = GWIDTH - GHOSTS * SLOTS
-    near_ref[:, GHOSTS * SLOTS :] = jnp.full((8, spare), 5000.0, F32)
-    nf_ref[GHOSTS * SLOTS :, :] = jnp.zeros((spare, K), BF16)
+    near_ref[:, :, GHOSTS * SLOTS :] = jnp.full((2, 8, spare), 5000.0, F32)
+    nf_ref[:, GHOSTS * SLOTS :, :] = jnp.zeros((2, spare, K), BF16)
     gnear_ref[...] = jnp.zeros_like(gnear_ref)
     gfeat_ref[...] = jnp.zeros_like(gfeat_ref)
     gpos_ref[...] = jnp.zeros_like(gpos_ref)
@@ -388,31 +407,38 @@
     def ghost_cell(cell, which):
         return flat(*(3 * at if side == 2 else side + 1 for side, at in zip(which, own_xyz(cell))))
 
-    def load_ghosts(cell):
+    def load_ghosts(cell, side=0):
         for g, which in enumerate(GHOST_LIST):
             spot = ghost_cell(cell, which)
-            nf_ref[g * SLOTS : (g + 1) * SLOTS, :] = feat_ref[spot]
+            nf_ref[side, g * SLOTS : (g + 1) * SLOTS, :] = feat_ref[spot]
             for k in range(3):
-                near_ref[k : k + 1, g * SLOTS : (g + 1) * SLOTS] = pos_ref[k, pl.ds(spot, 1), 0:SLOTS]
-
-    def geometry_at(cell):
-        return lambda block, tile: geometry_of(near_ref, ownpos_ref, cell, block, tile, False)
+                near_ref[side, k : k + 1, g * SLOTS : (g + 1) * SLOTS] = pos_ref[k, pl.ds(spot, 1), 0:SLOTS]
+
+    def geometry_at(cell, side=0):
+        return lambda block, tile: geometry_of(near_ref.at[side], ownpos_ref, cell, block, tile, False)
 
     at = 0
     for held in mom_in:
         mom_ref[at : at + held.shape[0]] = held[...]
         at += held.shape[0]
 
-    def forward(cell, carry):
-        load_ghosts(cell)
-        build_table(table_ref.at[cell], geometry_at(cell), GWIDTH // 128)
-        dens_ref[...] = jnp.dot(table_ref[cell], nf_ref[...], preferred_element_type=F32)
-        for block in range(2):
-            for m in range(NM):
-                mom_ref[cell, m, block * 16 : block * 16 + 16, :] += weigh(dens_ref, rw_ref, block, m)
+    def forward(pair, carry):
+        for side in range(2):
+            load_ghosts(pair * 2 + side, side)
+        for side in range(2):
+            cell = pair * 2 + side
+            build_table(table_ref.at[pair, side], geometry_at(cell, side), GWIDTH // 128)
+        for side in range(2):
+            dens_ref[side] = jnp.dot(table_ref[pair, side], nf_ref[side], preferred_element_type=F32)
+        for side in range(2):
+            cell = pair * 2 + side
+            for block in range(2):
+                for m in range(NM):
+                    rows = slice(block * 16, block * 16 + 16)
+                    mom_ref[cell, m, rows, :] += weigh(dens_ref.at[side], rw_ref, block, m)
         return carry
 
-    lax.fori_loop(0, CELLS, forward, 0)
+    lax.fori_loop(0, CELLS // 2, forward, 0)
 
     moments = [mom_ref[:, m].reshape(OWN, K) for m in range(NM)]
     product = moments[0]
@@ -450,25 +476,32 @@
         for k in range(3):
             gnear_ref[k : k + 1, tile * 128 : tile * 128 + 128] = sums[k]
 
-    def backward(cell, carry):
-        load_ghosts(cell)
-        spread(cot_ref, cell, rw_ref, dd_ref)
-        grads = lax.dot_general(
-            dd_ref[...], table_ref[cell], (((0,), (0,)), ((), ())), preferred_element_type=F32
-        ).T
-        for g, which in enumerate(GHOST_LIST):
-            gfeat_ref[ghost_cell(cell, which)] += grads[g * SLOTS : (g + 1) * SLOTS, :]
-        line = pair_forces(geometry_at(cell), dd_ref, nf_ref, dt_ref, GWIDTH, near_out, fown_ref)
-        oline_ref[pl.ds(cell, 1), :] = -line
-        for g, which in enumerate(GHOST_LIST):
-            spot = ghost_cell(cell, which)
-            for k in range(3):
-                gpos_ref[k, pl.ds(spot, 1), 0:SLOTS] += gnear_ref[
-                    k : k + 1, g * SLOTS : (g + 1) * SLOTS
-                ]
+    def backward(pair, carry):
+        for side in range(2):
+            cell = pair * 2 + side
+            load_ghosts(cell, side)
+            spread(cot_ref, cell, rw_ref, dd_ref.at[side])
+        parts = []
+        for side in range(2):
+            cell = pair * 2 + side
+            grads = lax.dot_general(
+                dd_ref[side], table_ref[pair, side], (((0,), (0,)), ((), ())), preferred_element_type=F32
+            ).T
+            for g, which in enumerate(GHOST_LIST):
+                gfeat_ref[ghost_cell(cell, which)] += grads[g * SLOTS : (g + 1) * SLOTS, :]
+            line = pair_forces(
+                geometry_at(cell, side), dd_ref.at[side], nf_ref.at[side], dt_ref, GWIDTH, near_out, fown_ref
+            )
+            oline_ref[pl.ds(cell, 1), :] = -line
+            for g, which in enumerate(GHOST_LIST):
+                spot = ghost_cell(cell, which)
+                for k in range(3):
+                    gpos_ref[k, pl.ds(spot, 1), 0:SLOTS] += gnear_ref[
+                        k : k + 1, g * SLOTS : (g + 1) * SLOTS
+                    ]
         return carry
 
-    lax.fori_loop(0, CELLS, backward, 0)
+    lax.fori_loop(0, CELLS // 2, backward, 0)
 
     for k in range(3):
         lines_ref[:, k * SLOTS : (k + 1) * SLOTS] = gpos_ref[k, :, 0:SLOTS]
@@ -574,8 +607,8 @@
             pltpu.VMEM((OWN, K), BF16),
             pltpu.VMEM((8, OWN), F32),
             pltpu.VMEM((3, OWN, 128), F32),
-            pltpu.VMEM((ROWS, OWN), BF16),
-            pltpu.VMEM((ROWS, K), F32),
+            pltpu.VMEM((2, ROWS, OWN), BF16),
+            pltpu.VMEM((2, ROWS, K), F32),
         ],
         flops=8 * count * ROWS * OWN * K,
     )[0]
@@ -591,11 +624,11 @@
             pltpu.VMEM((OWN, K), BF16),
             pltpu.VMEM((8, OWN), F32),
             pltpu.VMEM((3, OWN, 128), F32),
-            pltpu.VMEM((ROWS, OWN), BF16),
-            pltpu.VMEM((ROWS, K), BF16),
-            pltpu.VMEM((1, ROWS, 256), F32),
+            pltpu.VMEM((2, ROWS, OWN), BF16),
+            pltpu.VMEM((2, ROWS, K), BF16),
+            pltpu.VMEM((2, 1, ROWS, 256), F32),
             pltpu.VMEM((8, OWN), F32),
-            pltpu.VMEM((128, 128), F32),
+            pltpu.VMEM((2, 128, 128), F32),
             pltpu.VMEM((K, OWN), F32),
         ],
         flops=16 * count * ROWS * OWN * K,
@@ -615,16 +648,16 @@
             pltpu.VMEM((64, SLOTS, K), BF16),
             pltpu.VMEM((3, 64, 128), F32),
             pltpu.VMEM((64, 128), F32),
-            pltpu.VMEM((GWIDTH, K), BF16),
-            pltpu.VMEM((8, GWIDTH), F32),
+            pltpu.VMEM((2, GWIDTH, K), BF16),
+            pltpu.VMEM((2, 8, GWIDTH), F32),
             pltpu.VMEM((OWN, K), BF16),
             pltpu.VMEM((8, OWN), F32),
             pltpu.VMEM((3, OWN, 128), F32),
             pltpu.VMEM((OWN, 128), F32),
-            pltpu.VMEM((CELLS, ROWS, GWIDTH), BF16),
-            pltpu.VMEM((ROWS, K), F32),
+            pltpu.VMEM((CELLS // 2, 2, ROWS, GWIDTH), BF16),
+            pltpu.VMEM((2, ROWS, K), F32),
             pltpu.VMEM((CELLS, NM, SLOTS, K), F32),
-            pltpu.VMEM((ROWS, K), BF16),
+            pltpu.VMEM((2, ROWS, K), BF16),
             pltpu.VMEM((2, ROWS, 256), F32),
             pltpu.VMEM((8, GWIDTH), F32),
             pltpu.VMEM((128, 128), F32),
@@ -638,6 +671,42 @@
     )
 
 
+def first_payloads(counts, features, positions):
+    shapes = [((CELLS, ROW, K), BF16)] + faces(4)
+    anywhere = pl.BlockSpec(memory_space=pl.ANY)
+
+    def kernel(counts_in, feat_in, pos_in, *refs):
+        counts_ref, feat_ref, pos_ref, line_ref, sems = refs[3:]
+        copies = [
+            pltpu.make_async_copy(source, target, sems.at[k])
+            for k, (source, target) in enumerate(
+                ((counts_in, counts_ref), (pos_in, pos_ref), (feat_in, feat_ref))
+            )
+        ]
+        for copy in copies:
+            copy.start()
+        for copy in copies:
+            copy.wait()
+        pack_x_kernel(counts_ref, feat_ref, pos_ref, *refs[:3], line_ref)
+
+    return pl.pallas_call(
+        kernel,
+        out_shape=tuple(jax.ShapeDtypeStruct(shape, dtype) for shape, dtype in shapes),
+        in_specs=[anywhere] * 3,
+        out_specs=(VMEM_SPEC,) * 3,
+        scratch_shapes=[
+            pltpu.VMEM(counts.shape, counts.dtype),
+            pltpu.VMEM(features.shape, features.dtype),
+            pltpu.VMEM(positions.shape, positions.dtype),
+            pltpu.VMEM((CELLS, 128), F32),
+            pltpu.SemaphoreType.DMA((3,)),
+        ],
+        compiler_params=pltpu.CompilerParams(vmem_limit_bytes=16 * 1024 * 1024),
+        cost_estimate=pl.CostEstimate(flops=0, bytes_accessed=1 << 20, transcendentals=0),
+        name="pack_x",
+    )(counts, features, positions)
+
+
 def moved(lo, hi, axis, ring):
     size = lax.axis_size(axis)
     up = [(i, (i + 1) % size) for i in range(size if ring else size - 1)]
@@ -657,13 +726,8 @@
     plane = lax.axis_index("gz")
     edges = jnp.stack([plane == 0, plane == lax.axis_size("gz") - 1]).astype(jnp.int32)
     rw = jnp.transpose(radial_weight, (1, 0, 2))
-    own, xlo, xhi = call(
-        pack_x_kernel,
-        "pack_x",
-        [((CELLS, ROW, K), BF16)] + faces(4),
-        (counts, features.reshape(CELLS, SLOTS, K), jnp.transpose(positions, (0, 1, 3, 2, 4))),
-        scalars=1,
-        scratch=[pltpu.VMEM((CELLS, 128), F32)],
+    own, xlo, xhi = first_payloads(
+        counts, features.reshape(CELLS, SLOTS, K), jnp.transpose(positions, (0, 1, 3, 2, 4))
     )
     xs = moved(xlo, xhi, "gx", True)
     moms = [own_forward(own, rw, *FORWARD_PARTS[0])]

time: 97.8 us -> 91 us (0.930)
  Pallas kernels: 52.9 us -> 44.2 us
  waiting for transfers between devices: 12.3 us -> 13.9 us
    pallas_call x13 -> x12, Pallas kernels: 52.9 us -> 43.9 us  [call(): pl.pallas_call(kernel, out_shape=out_shape, in_specs=[SMEM_SPEC] * scalar...]
    ppermute x12, waiting for transfers between devices: 12.3 us -> 13.9 us  [moved(): return (lax.ppermute(hi, axis, up), lax.ppermute(lo, axis, down))]
  transfers between devices with their start and end apart: 12 -> 12, of which waited for: 4 -> 4; matrix products, arithmetic and copies ran while one was open for 0% -> 0% of each run, Pallas kernels for 17% -> 15%
where the time goes in v2:
time: 91 us; the launch traced here: 90.6 us
  Pallas kernels  44.2 us (49%)
  starting transfers between devices  28.7 us (32%)
  waiting for transfers between devices  13.9 us (15%)
  local copies, waits for them, and re-layouts  2.96 us (3%)
    pallas_call x12, Pallas kernels, call(): pl.pallas_call(kernel, out_shape=out_shape, in_specs=[SMEM_SPEC] * scalar...  43.9 us
    ppermute x12, starting transfers between devices, moved(): return (lax.ppermute(hi, axis, up), lax.ppermute(lo, axis, down))  28.7 us
    ppermute x12, waiting for transfers between devices, moved(): return (lax.ppermute(hi, axis, up), lax.ppermute(lo, axis, down))  13.9 us
    unnamed x20, local copies, waits for them, and re-layouts  2.96 us
  transfers between devices with their start and end apart: 12, of which 4 were waited for; matrix products, arithmetic and copies ran while one was open for 0% of the time, Pallas kernels for 15%

profile of v2, /device:TPU:8, one launch (start us, length us, event | category | flops | bytes accessed | tf_op | source)
XLA Modules:
  0.0 90.6 jit_solution(2109748833084265804)
XLA Ops:
  0.6 0.8 copy-done
  1.5 0.7 copy-done.1
  2.2 0.7 copy-done.2
  2.9 0.3 pack_x.1
  3.2 2.0 %collective-permute-start = (bf16[4,48,128]{2,1,0:T(8,128)(2,1)S(1)}, bf16[4,48,128]{2,1,0:T(8,128)(2,1)S(1)}, u32[]{:S(2)}, u32[]{:S(2)}) collective-permute-start(bf16[4,48,128]{2,1,0:T(8,128)(2,1)S(1)} %get-tuple-element.41), channel_id=1, source_target_pairs={{0,16},{16,32},{32,48},{48,64},{64,80},{80,96},{96,112},{112,128},... | collective-permute-start | bytes 147464 | tf_op jit(solution)/shard_map/ppermute | solution.py:714
  5.2 5.8 %collective-permute-start.1 = (bf16[4,48,128]{2,1,0:T(8,128)(2,1)S(1)}, bf16[4,48,128]{2,1,0:T(8,128)(2,1)S(1)}, u32[]{:S(2)}, u32[]{:S(2)}) collective-permute-start(bf16[4,48,128]{2,1,0:T(8,128)(2,1)S(1)} %get-tuple-element.42), channel_id=1, source_target_pairs={{16,0},{32,16},{48,32},{64,48},{80,64},{96,80},{112,96},{128,112},... | collective-permute-start | bytes 147464 | tf_op jit(solution)/shard_map/ppermute | solution.py:714
  10.9 0.7 copy-done.6
  11.6 1.2 %own_forward.3.refs_9_ = f32[2,9,32,128]{3,2,1,0:T(8,128)S(1)} custom-call(bf16[8,48,128]{2,1,0:T(8,128)(2,1)S(1)} %get-tuple-element.70.own_ref.own.refs_2_, f32[3,8,128]{2,1,0:T(8,128)S(1)} %bitcast.11), custom_call_target="tpu_custom_call" | custom-call | flops 1207959552 | bytes 1048576 | tf_op jit(solution)/shard_map/own_forward/pallas_call | solution.py:584
  12.8 0.1 add_convert_fusion.refs_1_
  12.9 2.8 %collective-permute-start.3 = (bf16[8,48,128]{2,1,0:T(8,128)(2,1)S(1)}, bf16[8,48,128]{2,1,0:T(8,128)(2,1)S(1)}, u32[]{:S(2)}, u32[]{:S(2)}) collective-permute-start(bf16[8,48,128]{2,1,0:T(8,128)(2,1)S(1)} %get-tuple-element.46), channel_id=1, source_target_pairs={{4,0},{8,4},{12,8},{0,12},{5,1},{9,5},{13,9},{1,13},{6,2},{10,6},{... | collective-permute-start | bytes 294920 | tf_op jit(solution)/shard_map/ppermute | solution.py:714
  15.8 1.2 %own_forward.4.refs_10_ = f32[2,9,32,128]{3,2,1,0:T(8,128)S(1)} custom-call(bf16[8,48,128]{2,1,0:T(8,128)(2,1)S(1)} %get-tuple-element.70.own_ref.own.refs_2_, f32[3,8,128]{2,1,0:T(8,128)S(1)} %bitcast.12), custom_call_target="tpu_custom_call" | custom-call | flops 1207959552 | bytes 1048576 | tf_op jit(solution)/shard_map/own_forward/pallas_call | solution.py:584
  17.0 4.6 %collective-permute-done.2.ylo.refs_5_ = bf16[8,48,128]{2,1,0:T(8,128)(2,1)S(1)} collective-permute-done((bf16[8,48,128]{2,1,0:T(8,128)(2,1)S(1)}, bf16[8,48,128]{2,1,0:T(8,128)(2,1)S(1)}, u32[]{:S(2)}, u32[]{:S(2)}) %collective-permute-start.2) | collective-permute-done | bytes 98336 | tf_op jit(solution)/shard_map/ppermute | solution.py:714
  21.6 1.9 %collective-permute-start.5 = (bf16[16,48,128]{2,1,0:T(8,128)(2,1)S(1)}, bf16[16,48,128]{2,1,0:T(8,128)(2,1)S(1)}, u32[]{:S(2)}, u32[]{:S(2)}) collective-permute-start(bf16[16,48,128]{2,1,0:T(8,128)(2,1)S(1)} %get-tuple-element.51), channel_id=1, source_target_pairs={{1,0},{2,1},{3,2},{5,4},{6,5},{7,6},{9,8},{10,9},{11,10},{13,12},{... | collective-permute-start | bytes 589832 | tf_op jit(solution)/shard_map/ppermute | solution.py:714
  23.6 0.0 copy-start.4
  23.6 0.0 copy-start.5
  23.6 2.7 %collective-permute-start.4 = (bf16[16,48,128]{2,1,0:T(8,128)(2,1)S(1)}, bf16[16,48,128]{2,1,0:T(8,128)(2,1)S(1)}, u32[]{:S(2)}, u32[]{:S(2)}) collective-permute-start(bf16[16,48,128]{2,1,0:T(8,128)(2,1)S(1)} %get-tuple-element.50), channel_id=1, source_target_pairs={{0,1},{1,2},{2,3},{4,5},{5,6},{6,7},{8,9},{9,10},{10,11},{12,13},{... | collective-permute-start | bytes 589832 | tf_op jit(solution)/shard_map/ppermute | solution.py:714
  26.4 2.1 %own_forward.5.refs_11_ = f32[4,9,32,128]{3,2,1,0:T(8,128)S(1)} custom-call(bf16[8,48,128]{2,1,0:T(8,128)(2,1)S(1)} %get-tuple-element.70.own_ref.own.refs_2_, f32[3,8,128]{2,1,0:T(8,128)S(1)} %bitcast.13), custom_call_target="tpu_custom_call" | custom-call | flops 2415919104 | bytes 1048576 | tf_op jit(solution)/shard_map/own_forward/pallas_call | solution.py:584
  28.4 2.3 %collective-permute-done.4.refs_7_ = bf16[16,48,128]{2,1,0:T(8,128)(2,1)S(1)} collective-permute-done((bf16[16,48,128]{2,1,0:T(8,128)(2,1)S(1)}, bf16[16,48,128]{2,1,0:T(8,128)(2,1)S(1)}, u32[]{:S(2)}, u32[]{:S(2)}) %collective-permute-start.4) | collective-permute-done | bytes 196640 | tf_op jit(solution)/shard_map/ppermute | solution.py:714
  30.8 28.6 %ghost.1 = (bf16[256,128]{1,0:T(8,128)(2,1)}, bf16[16,48,128]{2,1,0:T(8,128)(2,1)S(1)}, bf16[16,48,128]{2,1,0:T(8,128)(2,1)S(1)}, f32[32,32,128]{2,1,0:T(8,128)S...) custom-call(s32[2,2,2]{2,1,0:T(2,128)S(1)} %copy-done.3, s32[2]{0:T(128)S(1)} %add_convert_fusion.refs_1_, ...), custom_call_target="tpu_custom_call" | custom-call | flops 24159191040 | bytes 1048576 | tf_op jit(solution)/shard_map/ghost/pallas_call | solution.py:584
  59.4 1.9 %collective-permute-start.6 = (bf16[16,48,128]{2,1,0:T(8,128)(2,1)S(1)}, bf16[16,48,128]{2,1,0:T(8,128)(2,1)S(1)}, u32[]{:S(2)}, u32[]{:S(2)}) collective-permute-start(bf16[16,48,128]{2,1,0:T(8,128)(2,1)S(1)} %get-tuple-element.56), channel_id=1, source_target_pairs={{0,1},{1,2},{2,3},{4,5},{5,6},{6,7},{8,9},{9,10},{10,11},{12,13},{... | collective-permute-start | bytes 589832 | tf_op jit(solution)/shard_map/ppermute | solution.py:714
  61.3 3.6 %collective-permute-start.7 = (bf16[16,48,128]{2,1,0:T(8,128)(2,1)S(1)}, bf16[16,48,128]{2,1,0:T(8,128)(2,1)S(1)}, u32[]{:S(2)}, u32[]{:S(2)}) collective-permute-start(bf16[16,48,128]{2,1,0:T(8,128)(2,1)S(1)} %get-tuple-element.57), channel_id=1, source_target_pairs={{1,0},{2,1},{3,2},{5,4},{6,5},{7,6},{9,8},{10,9},{11,10},{13,12},{... | collective-permute-start | bytes 589832 | tf_op jit(solution)/shard_map/ppermute | solution.py:714
  64.9 4.5 %own_backward.3 = (f32[256,128]{1,0:T(8,128)S(1)}, f32[8,128]{1,0:T(8,128)S(1)}) custom-call(bf16[8,48,128]{2,1,0:T(8,128)(2,1)S(1)} %get-tuple-element.70.own_ref.own.refs_2_, f32[3,8,128]{2,1,0:T(8,128)S(1)} %bitcast.15, f32[8,9,32,128]{3,2,1,0:T(8,128)S(1)} %get-tuple-element.58.mom_ref), custom_call_target="tpu_custom_call" | custom-call | flops 4831838208 | bytes 1048576 | tf_op jit(solution)/shard_map/own_backward/pallas_call | solution.py:584
  69.5 0.1 back_y.1
  69.6 0.1 collective-permute-start.9
  69.6 2.0 %collective-permute-start.8 = (bf16[8,48,128]{2,1,0:T(8,128)(2,1)S(1)}, bf16[8,48,128]{2,1,0:T(8,128)(2,1)S(1)}, u32[]{:S(2)}, u32[]{:S(2)}) collective-permute-start(bf16[8,48,128]{2,1,0:T(8,128)(2,1)S(1)} %get-tuple-element.62), channel_id=1, source_target_pairs={{0,4},{4,8},{8,12},{12,0},{1,5},{5,9},{9,13},{13,1},{2,6},{6,10},{... | collective-permute-start | bytes 294920 | tf_op jit(solution)/shard_map/ppermute | solution.py:714
  71.7 2.4 %own_backward.4 = (f32[256,128]{1,0:T(8,128)S(1)}, f32[8,128]{1,0:T(8,128)S(1)}) custom-call(bf16[8,48,128]{2,1,0:T(8,128)(2,1)S(1)} %get-tuple-element.70.own_ref.own.refs_2_, f32[3,8,128]{2,1,0:T(8,128)S(1)} %bitcast.16, f32[8,9,32,128]{3,2,1,0:T(8,128)S(1)} %get-tuple-element.58.mom_ref), custom_call_target="tpu_custom_call" | custom-call | flops 2415919104 | bytes 1048576 | tf_op jit(solution)/shard_map/own_backward/pallas_call | solution.py:584
  74.0 1.7 %collective-permute-done.8.ylo.refs_5_ = bf16[8,48,128]{2,1,0:T(8,128)(2,1)S(1)} collective-permute-done((bf16[8,48,128]{2,1,0:T(8,128)(2,1)S(1)}, bf16[8,48,128]{2,1,0:T(8,128)(2,1)S(1)}, u32[]{:S(2)}, u32[]{:S(2)}) %collective-permute-start.8) | collective-permute-done | bytes 98336 | tf_op jit(solution)/shard_map/ppermute | solution.py:714
  75.8 0.1 back_x.1
  75.8 5.8 %collective-permute-start.11 = (bf16[4,48,128]{2,1,0:T(8,128)(2,1)S(1)}, bf16[4,48,128]{2,1,0:T(8,128)(2,1)S(1)}, u32[]{:S(2)}, u32[]{:S(2)}) collective-permute-start(bf16[4,48,128]{2,1,0:T(8,128)(2,1)S(1)} %get-tuple-element.69), channel_id=1, source_target_pairs={{16,0},{32,16},{48,32},{64,48},{80,64},{96,80},{112,96},{128,112},... | collective-permute-start | bytes 147464 | tf_op jit(solution)/shard_map/ppermute | solution.py:714
  81.6 2.4 %own_backward.5 = (f32[256,128]{1,0:T(8,128)S(1)}, f32[8,128]{1,0:T(8,128)S(1)}) custom-call(bf16[8,48,128]{2,1,0:T(8,128)(2,1)S(1)} %get-tuple-element.70.own_ref.own.refs_2_, f32[3,8,128]{2,1,0:T(8,128)S(1)} %bitcast.17, f32[8,9,32,128]{3,2,1,0:T(8,128)S(1)} %get-tuple-element.58.mom_ref), custom_call_target="tpu_custom_call" | custom-call | flops 2415919104 | bytes 1048576 | tf_op jit(solution)/shard_map/own_backward/pallas_call | solution.py:584
  84.0 5.3 %collective-permute-done.10.refs_7_ = bf16[4,48,128]{2,1,0:T(8,128)(2,1)S(1)} collective-permute-done((bf16[4,48,128]{2,1,0:T(8,128)(2,1)S(1)}, bf16[4,48,128]{2,1,0:T(8,128)(2,1)S(1)}, u32[]{:S(2)}, u32[]{:S(2)}) %collective-permute-start.10) | collective-permute-done | bytes 49184 | tf_op jit(solution)/shard_map/ppermute | solution.py:714
  89.3 1.3 %finish.1 = (f32[8,32,128]{2,1,0:T(8,128)}, f32[2,2,3,2,32]{4,3,2,1,0:T(2,128)}) custom-call(s32[2,2,2]{2,1,0:T(2,128)S(1)} %copy-done.3, f32[32,32,128]{2,1,0:T(8,128)S(1)} %get-tuple-element.54.rest_ref.refs_1_, f32[32,128]{1,0:T(8,128)S(1)} %get-tuple-element.55.rlines_ref.refs_2_, bf16[16,48,128]{2,1,0:T(8,128)(2,1)S(1)} %collective-permute-done.6.zlo.refs_3_, ...), custom_call_target="tpu_custom_call" | custom-call | bytes 1048576 | tf_op jit(solution)/shard_map/finish/pallas_call | solution.py:584
  (26 shorter events, 0.1 us)
Async XLA Ops:
  0.6 0.8 copy-start
  1.5 0.7 copy-start.1
  2.2 0.7 copy-start.2
  3.2 9.7 %collective-permute-start = (bf16[4,48,128]{2,1,0:T(8,128)(2,1)S(1)}, bf16[4,48,128]{2,1,0:T(8,128)(2,1)S(1)}, u32[]{:S(2)}, u32[]{:S(2)}) collective-permute-start(bf16[4,48,128]{2,1,0:T(8,128)(2,1)S(1)} %get-tuple-element.41), channel_id=1, source_target_pairs={{0,16},{16,32},{32,48},{48,64},{64,80},{80,96},{96,112},{112,128},... | collective-permute-start | bytes 147464 | tf_op jit(solution)/shard_map/ppermute | solution.py:714
  5.2 7.8 %collective-permute-start.1 = (bf16[4,48,128]{2,1,0:T(8,128)(2,1)S(1)}, bf16[4,48,128]{2,1,0:T(8,128)(2,1)S(1)}, u32[]{:S(2)}, u32[]{:S(2)}) collective-permute-start(bf16[4,48,128]{2,1,0:T(8,128)(2,1)S(1)} %get-tuple-element.42), channel_id=1, source_target_pairs={{16,0},{32,16},{48,32},{64,48},{80,64},{96,80},{112,96},{128,112},... | collective-permute-start | bytes 147464 | tf_op jit(solution)/shard_map/ppermute | solution.py:714
  10.9 0.7 copy-start.6
  11.6 4.2 %copy-start.7 = (f32[8,3,128]{2,0,1:T(8,128)S(1)}, f32[8,3,128]{2,0,1:T(8,128)}, u32[]{:S(2)}) copy-start(f32[8,3,128]{2,0,1:T(8,128)} %param.12) | copy-start | bytes 36868
  12.9 8.7 %collective-permute-start.3 = (bf16[8,48,128]{2,1,0:T(8,128)(2,1)S(1)}, bf16[8,48,128]{2,1,0:T(8,128)(2,1)S(1)}, u32[]{:S(2)}, u32[]{:S(2)}) collective-permute-start(bf16[8,48,128]{2,1,0:T(8,128)(2,1)S(1)} %get-tuple-element.46), channel_id=1, source_target_pairs={{4,0},{8,4},{12,8},{0,12},{5,1},{9,5},{13,9},{1,13},{6,2},{10,6},{... | collective-permute-start | bytes 294920 | tf_op jit(solution)/shard_map/ppermute | solution.py:714
  15.8 5.8 %collective-permute-start.2 = (bf16[8,48,128]{2,1,0:T(8,128)(2,1)S(1)}, bf16[8,48,128]{2,1,0:T(8,128)(2,1)S(1)}, u32[]{:S(2)}, u32[]{:S(2)}) collective-permute-start(bf16[8,48,128]{2,1,0:T(8,128)(2,1)S(1)} %get-tuple-element.45), channel_id=1, source_target_pairs={{0,4},{4,8},{8,12},{12,0},{1,5},{5,9},{9,13},{13,1},{2,6},{6,10},{... | collective-permute-start | bytes 294920 | tf_op jit(solution)/shard_map/ppermute | solution.py:714
  21.6 9.1 %collective-permute-start.5 = (bf16[16,48,128]{2,1,0:T(8,128)(2,1)S(1)}, bf16[16,48,128]{2,1,0:T(8,128)(2,1)S(1)}, u32[]{:S(2)}, u32[]{:S(2)}) collective-permute-start(bf16[16,48,128]{2,1,0:T(8,128)(2,1)S(1)} %get-tuple-element.51), channel_id=1, source_target_pairs={{1,0},{2,1},{3,2},{5,4},{6,5},{7,6},{9,8},{10,9},{11,10},{13,12},{... | collective-permute-start | bytes 589832 | tf_op jit(solution)/shard_map/ppermute | solution.py:714
  23.6 7.2 %copy-start.3 = (s32[2,2,2]{2,1,0:T(2,128)S(1)}, s32[2,2,2]{2,1,0:T(2,128)}, u32[]{:S(2)}) copy-start(s32[2,2,2]{2,1,0:T(2,128)} %refs_0_.3) | copy-start | bytes 100
  23.6 7.2 %copy-start.4 = (bf16[5,128,128]{2,1,0:T(8,128)(2,1)S(1)}, bf16[5,128,128]{2,1,0:T(8,128)(2,1)}, u32[]{:S(2)}) copy-start(bf16[5,128,128]{2,1,0:T(8,128)(2,1)} %refs_15_.1) | copy-start | bytes 491524
  23.6 7.2 %copy-start.5 = (bf16[128,128]{1,0:T(8,128)(2,1)S(1)}, bf16[128,128]{1,0:T(8,128)(2,1)}, u32[]{:S(2)}) copy-start(bf16[128,128]{1,0:T(8,128)(2,1)} %refs_14_.1) | copy-start | bytes 98308
  23.6 7.2 %copy-start.8 = (s32[2,2,2,32]{3,2,1,0:T(2,128)S(1)}, s32[2,2,2,32]{3,2,1,0:T(2,128)}, u32[]{:S(2)}) copy-start(s32[2,2,2,32]{3,2,1,0:T(2,128)} %param.11) | copy-start | bytes 3076
  23.6 7.2 %copy-start.9 = (f32[5,128]{1,0:T(8,128)S(1)}, f32[5,128]{1,0:T(8,128)}, u32[]{:S(2)}) copy-start(f32[5,128]{1,0:T(8,128)} %refs_16_.1) | copy-start | bytes 7684
  23.6 7.1 %collective-permute-start.4 = (bf16[16,48,128]{2,1,0:T(8,128)(2,1)S(1)}, bf16[16,48,128]{2,1,0:T(8,128)(2,1)S(1)}, u32[]{:S(2)}, u32[]{:S(2)}) collective-permute-start(bf16[16,48,128]{2,1,0:T(8,128)(2,1)S(1)} %get-tuple-element.50), channel_id=1, source_target_pairs={{0,1},{1,2},{2,3},{4,5},{5,6},{6,7},{8,9},{9,10},{10,11},{12,13},{... | collective-permute-start | bytes 589832 | tf_op jit(solution)/shard_map/ppermute | solution.py:714
  59.4 10.1 %collective-permute-start.6 = (bf16[16,48,128]{2,1,0:T(8,128)(2,1)S(1)}, bf16[16,48,128]{2,1,0:T(8,128)(2,1)S(1)}, u32[]{:S(2)}, u32[]{:S(2)}) collective-permute-start(bf16[16,48,128]{2,1,0:T(8,128)(2,1)S(1)} %get-tuple-element.56), channel_id=1, source_target_pairs={{0,1},{1,2},{2,3},{4,5},{5,6},{6,7},{8,9},{9,10},{10,11},{12,13},{... | collective-permute-start | bytes 589832 | tf_op jit(solution)/shard_map/ppermute | solution.py:714
  61.3 8.2 %collective-permute-start.7 = (bf16[16,48,128]{2,1,0:T(8,128)(2,1)S(1)}, bf16[16,48,128]{2,1,0:T(8,128)(2,1)S(1)}, u32[]{:S(2)}, u32[]{:S(2)}) collective-permute-start(bf16[16,48,128]{2,1,0:T(8,128)(2,1)S(1)} %get-tuple-element.57), channel_id=1, source_target_pairs={{1,0},{2,1},{3,2},{5,4},{6,5},{7,6},{9,8},{10,9},{11,10},{13,12},{... | collective-permute-start | bytes 589832 | tf_op jit(solution)/shard_map/ppermute | solution.py:714
  69.6 6.2 %collective-permute-start.9 = (bf16[8,48,128]{2,1,0:T(8,128)(2,1)S(1)}, bf16[8,48,128]{2,1,0:T(8,128)(2,1)S(1)}, u32[]{:S(2)}, u32[]{:S(2)}) collective-permute-start(bf16[8,48,128]{2,1,0:T(8,128)(2,1)S(1)} %get-tuple-element.63), channel_id=1, source_target_pairs={{4,0},{8,4},{12,8},{0,12},{5,1},{9,5},{13,9},{1,13},{6,2},{10,6},{... | collective-permute-start | bytes 294920 | tf_op jit(solution)/shard_map/ppermute | solution.py:714
  69.6 6.1 %collective-permute-start.8 = (bf16[8,48,128]{2,1,0:T(8,128)(2,1)S(1)}, bf16[8,48,128]{2,1,0:T(8,128)(2,1)S(1)}, u32[]{:S(2)}, u32[]{:S(2)}) collective-permute-start(bf16[8,48,128]{2,1,0:T(8,128)(2,1)S(1)} %get-tuple-element.62), channel_id=1, source_target_pairs={{0,4},{4,8},{8,12},{12,0},{1,5},{5,9},{9,13},{13,1},{2,6},{6,10},{... | collective-permute-start | bytes 294920 | tf_op jit(solution)/shard_map/ppermute | solution.py:714
  75.8 13.5 %collective-permute-start.11 = (bf16[4,48,128]{2,1,0:T(8,128)(2,1)S(1)}, bf16[4,48,128]{2,1,0:T(8,128)(2,1)S(1)}, u32[]{:S(2)}, u32[]{:S(2)}) collective-permute-start(bf16[4,48,128]{2,1,0:T(8,128)(2,1)S(1)} %get-tuple-element.69), channel_id=1, source_target_pairs={{16,0},{32,16},{48,32},{64,48},{80,64},{96,80},{112,96},{128,112},... | collective-permute-start | bytes 147464 | tf_op jit(solution)/shard_map/ppermute | solution.py:714
  81.6 7.7 %collective-permute-start.10 = (bf16[4,48,128]{2,1,0:T(8,128)(2,1)S(1)}, bf16[4,48,128]{2,1,0:T(8,128)(2,1)S(1)}, u32[]{:S(2)}, u32[]{:S(2)}) collective-permute-start(bf16[4,48,128]{2,1,0:T(8,128)(2,1)S(1)} %get-tuple-element.68), channel_id=1, source_target_pairs={{0,16},{16,32},{32,48},{48,64},{64,80},{80,96},{96,112},{112,128},... | collective-permute-start | bytes 147464 | tf_op jit(solution)/shard_map/ppermute | solution.py:714

commit v3 on v2

--- a/solution.py
+++ b/solution.py
@@ -701,7 +701,7 @@
             pltpu.VMEM((CELLS, 128), F32),
             pltpu.SemaphoreType.DMA((3,)),
         ],
-        compiler_params=pltpu.CompilerParams(vmem_limit_bytes=16 * 1024 * 1024),
+        compiler_params=pltpu.CompilerParams(vmem_limit_bytes=60 * 1024 * 1024),
         cost_estimate=pl.CostEstimate(flops=0, bytes_accessed=1 << 20, transcendentals=0),
         name="pack_x",
     )(counts, features, positions)

time: 91 us -> 90.4 us (level)
  Pallas kernels: 44.2 us -> 45.6 us
  local copies, waits for them, and re-layouts: 2.96 us -> 1.64 us
    pallas_call x1, Pallas kernels: 0.3 us -> 1.73 us  [first_payloads(): pl.pallas_call(kernel, out_shape=tuple((jax.ShapeDtypeStruct(shape, dtype...]
    unnamed x20 -> x18, local copies, waits for them, and re-layouts: 2.96 us -> 1.64 us
where the time goes in v3:
time: 90.4 us; the launch traced here: 90.1 us
  Pallas kernels  45.6 us (50%)
  starting transfers between devices  28 us (31%)
  waiting for transfers between devices  13.9 us (15%)
  local copies, waits for them, and re-layouts  1.64 us (2%)
    pallas_call x12, Pallas kernels, call(): pl.pallas_call(kernel, out_shape=out_shape, in_specs=[SMEM_SPEC] * scalar...  43.9 us
    ppermute x12, starting transfers between devices, moved(): return (lax.ppermute(hi, axis, up), lax.ppermute(lo, axis, down))  28 us
    ppermute x12, waiting for transfers between devices, moved(): return (lax.ppermute(hi, axis, up), lax.ppermute(lo, axis, down))  13.9 us
  transfers between devices with their start and end apart: 12, of which 4 were waited for; matrix products, arithmetic and copies ran while one was open for 0% of the time, Pallas kernels for 15%

profile of v3, /device:TPU:8, one launch (start us, length us, event | category | flops | bytes accessed | tf_op | source)
XLA Modules:
  0.0 90.1 jit_solution(15957538098158945969)
XLA Ops:
  0.6 1.7 %pack_x.1 = (bf16[8,48,128]{2,1,0:T(8,128)(2,1)}, bf16[4,48,128]{2,1,0:T(8,128)(2,1)}, bf16[4,48,128]{2,1,0:T(8,128)(2,1)}) custom-call(s32[2,2,2]{2,1,0:T(2,128)} %refs_0_.3, bf16[8,32,128]{2,1,0:T(8,128)(2,1)} %bitcast.17, f32[2,2,3,2,32]{4,3,2,1,0:T(2,128)} %bitcast.18), custom_call_target="tpu_custom_call" | custom-call | bytes 1048576 | tf_op jit(solution)/shard_map/pack_x/pallas_call | solution.py:692
  2.4 2.0 %collective-permute-start = (bf16[4,48,128]{2,1,0:T(8,128)(2,1)}, bf16[4,48,128]{2,1,0:T(8,128)(2,1)S(1)}, u32[]{:S(2)}, u32[]{:S(2)}) collective-permute-start(bf16[4,48,128]{2,1,0:T(8,128)(2,1)} %get-tuple-element.41), channel_id=1, source_target_pairs={{0,16},{16,32},{32,48},{48,64},{64,80},{80,96},{96,112},{112,128},... | collective-permute-start | bytes 147464 | tf_op jit(solution)/shard_map/ppermute | solution.py:714
  4.4 5.8 %collective-permute-start.1 = (bf16[4,48,128]{2,1,0:T(8,128)(2,1)}, bf16[4,48,128]{2,1,0:T(8,128)(2,1)S(1)}, u32[]{:S(2)}, u32[]{:S(2)}) collective-permute-start(bf16[4,48,128]{2,1,0:T(8,128)(2,1)} %get-tuple-element.42), channel_id=1, source_target_pairs={{16,0},{32,16},{48,32},{64,48},{80,64},{96,80},{112,96},{128,112},... | collective-permute-start | bytes 147464 | tf_op jit(solution)/shard_map/ppermute | solution.py:714
  10.1 0.9 copy-done
  11.0 0.7 copy-done.5
  11.7 1.2 %own_forward.3.refs_9_ = f32[2,9,32,128]{3,2,1,0:T(8,128)S(1)} custom-call(bf16[8,48,128]{2,1,0:T(8,128)(2,1)S(1)} %copy-done, f32[3,8,128]{2,1,0:T(8,128)S(1)} %bitcast.9), custom_call_target="tpu_custom_call" | custom-call | flops 1207959552 | bytes 1048576 | tf_op jit(solution)/shard_map/own_forward/pallas_call | solution.py:584
  12.9 0.1 add_convert_fusion.refs_1_
  13.0 2.8 %collective-permute-start.3 = (bf16[8,48,128]{2,1,0:T(8,128)(2,1)S(1)}, bf16[8,48,128]{2,1,0:T(8,128)(2,1)S(1)}, u32[]{:S(2)}, u32[]{:S(2)}) collective-permute-start(bf16[8,48,128]{2,1,0:T(8,128)(2,1)S(1)} %get-tuple-element.46), channel_id=1, source_target_pairs={{4,0},{8,4},{12,8},{0,12},{5,1},{9,5},{13,9},{1,13},{6,2},{10,6},{... | collective-permute-start | bytes 294920 | tf_op jit(solution)/shard_map/ppermute | solution.py:714
  15.9 1.2 %own_forward.4.refs_10_ = f32[2,9,32,128]{3,2,1,0:T(8,128)S(1)} custom-call(bf16[8,48,128]{2,1,0:T(8,128)(2,1)S(1)} %copy-done, f32[3,8,128]{2,1,0:T(8,128)S(1)} %bitcast.10), custom_call_target="tpu_custom_call" | custom-call | flops 1207959552 | bytes 1048576 | tf_op jit(solution)/shard_map/own_forward/pallas_call | solution.py:584
  17.1 4.6 %collective-permute-done.2.ylo.refs_5_ = bf16[8,48,128]{2,1,0:T(8,128)(2,1)S(1)} collective-permute-done((bf16[8,48,128]{2,1,0:T(8,128)(2,1)S(1)}, bf16[8,48,128]{2,1,0:T(8,128)(2,1)S(1)}, u32[]{:S(2)}, u32[]{:S(2)}) %collective-permute-start.2) | collective-permute-done | bytes 98336 | tf_op jit(solution)/shard_map/ppermute | solution.py:714
  21.7 1.9 %collective-permute-start.5 = (bf16[16,48,128]{2,1,0:T(8,128)(2,1)S(1)}, bf16[16,48,128]{2,1,0:T(8,128)(2,1)S(1)}, u32[]{:S(2)}, u32[]{:S(2)}) collective-permute-start(bf16[16,48,128]{2,1,0:T(8,128)(2,1)S(1)} %get-tuple-element.51), channel_id=1, source_target_pairs={{1,0},{2,1},{3,2},{5,4},{6,5},{7,6},{9,8},{10,9},{11,10},{13,12},{... | collective-permute-start | bytes 589832 | tf_op jit(solution)/shard_map/ppermute | solution.py:714
  23.7 0.0 copy-start.1
  23.7 0.0 copy-start.2
  23.7 0.0 copy-start.4
  23.7 0.0 copy-start.6
  23.7 2.7 %collective-permute-start.4 = (bf16[16,48,128]{2,1,0:T(8,128)(2,1)S(1)}, bf16[16,48,128]{2,1,0:T(8,128)(2,1)S(1)}, u32[]{:S(2)}, u32[]{:S(2)}) collective-permute-start(bf16[16,48,128]{2,1,0:T(8,128)(2,1)S(1)} %get-tuple-element.50), channel_id=1, source_target_pairs={{0,1},{1,2},{2,3},{4,5},{5,6},{6,7},{8,9},{9,10},{10,11},{12,13},{... | collective-permute-start | bytes 589832 | tf_op jit(solution)/shard_map/ppermute | solution.py:714
  26.5 2.1 %own_forward.5.refs_11_ = f32[4,9,32,128]{3,2,1,0:T(8,128)S(1)} custom-call(bf16[8,48,128]{2,1,0:T(8,128)(2,1)S(1)} %copy-done, f32[3,8,128]{2,1,0:T(8,128)S(1)} %bitcast.11), custom_call_target="tpu_custom_call" | custom-call | flops 2415919104 | bytes 1048576 | tf_op jit(solution)/shard_map/own_forward/pallas_call | solution.py:584
  28.5 2.3 %collective-permute-done.4.refs_7_ = bf16[16,48,128]{2,1,0:T(8,128)(2,1)S(1)} collective-permute-done((bf16[16,48,128]{2,1,0:T(8,128)(2,1)S(1)}, bf16[16,48,128]{2,1,0:T(8,128)(2,1)S(1)}, u32[]{:S(2)}, u32[]{:S(2)}) %collective-permute-start.4) | collective-permute-done | bytes 196640 | tf_op jit(solution)/shard_map/ppermute | solution.py:714
  30.9 28.6 %ghost.1 = (bf16[256,128]{1,0:T(8,128)(2,1)}, bf16[16,48,128]{2,1,0:T(8,128)(2,1)S(1)}, bf16[16,48,128]{2,1,0:T(8,128)(2,1)S(1)}, f32[32,32,128]{2,1,0:T(8,128)S...) custom-call(s32[2,2,2]{2,1,0:T(2,128)S(1)} %copy-done.2, s32[2]{0:T(128)S(1)} %add_convert_fusion.refs_1_, ...), custom_call_target="tpu_custom_call" | custom-call | flops 24159191040 | bytes 1048576 | tf_op jit(solution)/shard_map/ghost/pallas_call | solution.py:584
  59.5 1.9 %collective-permute-start.6 = (bf16[16,48,128]{2,1,0:T(8,128)(2,1)S(1)}, bf16[16,48,128]{2,1,0:T(8,128)(2,1)S(1)}, u32[]{:S(2)}, u32[]{:S(2)}) collective-permute-start(bf16[16,48,128]{2,1,0:T(8,128)(2,1)S(1)} %get-tuple-element.56), channel_id=1, source_target_pairs={{0,1},{1,2},{2,3},{4,5},{5,6},{6,7},{8,9},{9,10},{10,11},{12,13},{... | collective-permute-start | bytes 589832 | tf_op jit(solution)/shard_map/ppermute | solution.py:714
  61.4 3.6 %collective-permute-start.7 = (bf16[16,48,128]{2,1,0:T(8,128)(2,1)S(1)}, bf16[16,48,128]{2,1,0:T(8,128)(2,1)S(1)}, u32[]{:S(2)}, u32[]{:S(2)}) collective-permute-start(bf16[16,48,128]{2,1,0:T(8,128)(2,1)S(1)} %get-tuple-element.57), channel_id=1, source_target_pairs={{1,0},{2,1},{3,2},{5,4},{6,5},{7,6},{9,8},{10,9},{11,10},{13,12},{... | collective-permute-start | bytes 589832 | tf_op jit(solution)/shard_map/ppermute | solution.py:714
  65.1 4.5 %own_backward.3 = (f32[256,128]{1,0:T(8,128)S(1)}, f32[8,128]{1,0:T(8,128)S(1)}) custom-call(bf16[8,48,128]{2,1,0:T(8,128)(2,1)S(1)} %copy-done.1, f32[3,8,128]{2,1,0:T(8,128)S(1)} %bitcast.13, f32[8,9,32,128]{3,2,1,0:T(8,128)S(1)} %get-tuple-element.58.mom_ref), custom_call_target="tpu_custom_call" | custom-call | flops 4831838208 | bytes 1048576 | tf_op jit(solution)/shard_map/own_backward/pallas_call | solution.py:584
  69.6 0.1 back_y.1
  69.7 0.1 collective-permute-start.9
  69.8 2.0 %collective-permute-start.8 = (bf16[8,48,128]{2,1,0:T(8,128)(2,1)S(1)}, bf16[8,48,128]{2,1,0:T(8,128)(2,1)S(1)}, u32[]{:S(2)}, u32[]{:S(2)}) collective-permute-start(bf16[8,48,128]{2,1,0:T(8,128)(2,1)S(1)} %get-tuple-element.62), channel_id=1, source_target_pairs={{0,4},{4,8},{8,12},{12,0},{1,5},{5,9},{9,13},{13,1},{2,6},{6,10},{... | collective-permute-start | bytes 294920 | tf_op jit(solution)/shard_map/ppermute | solution.py:714
  71.8 2.4 %own_backward.4 = (f32[256,128]{1,0:T(8,128)S(1)}, f32[8,128]{1,0:T(8,128)S(1)}) custom-call(bf16[8,48,128]{2,1,0:T(8,128)(2,1)S(1)} %copy-done.1, f32[3,8,128]{2,1,0:T(8,128)S(1)} %bitcast.14, f32[8,9,32,128]{3,2,1,0:T(8,128)S(1)} %get-tuple-element.58.mom_ref), custom_call_target="tpu_custom_call" | custom-call | flops 2415919104 | bytes 1048576 | tf_op jit(solution)/shard_map/own_backward/pallas_call | solution.py:584
  74.2 1.7 %collective-permute-done.8.ylo.refs_5_ = bf16[8,48,128]{2,1,0:T(8,128)(2,1)S(1)} collective-permute-done((bf16[8,48,128]{2,1,0:T(8,128)(2,1)S(1)}, bf16[8,48,128]{2,1,0:T(8,128)(2,1)S(1)}, u32[]{:S(2)}, u32[]{:S(2)}) %collective-permute-start.8) | collective-permute-done | bytes 98336 | tf_op jit(solution)/shard_map/ppermute | solution.py:714
  75.9 0.1 back_x.1
  76.0 5.1 %collective-permute-start.11 = (bf16[4,48,128]{2,1,0:T(8,128)(2,1)S(1)}, bf16[4,48,128]{2,1,0:T(8,128)(2,1)S(1)}, u32[]{:S(2)}, u32[]{:S(2)}) collective-permute-start(bf16[4,48,128]{2,1,0:T(8,128)(2,1)S(1)} %get-tuple-element.69), channel_id=1, source_target_pairs={{16,0},{32,16},{48,32},{64,48},{80,64},{96,80},{112,96},{128,112},... | collective-permute-start | bytes 147464 | tf_op jit(solution)/shard_map/ppermute | solution.py:714
  81.1 2.4 %own_backward.5 = (f32[256,128]{1,0:T(8,128)S(1)}, f32[8,128]{1,0:T(8,128)S(1)}) custom-call(bf16[8,48,128]{2,1,0:T(8,128)(2,1)S(1)} %copy-done.1, f32[3,8,128]{2,1,0:T(8,128)S(1)} %bitcast.15, f32[8,9,32,128]{3,2,1,0:T(8,128)S(1)} %get-tuple-element.58.mom_ref), custom_call_target="tpu_custom_call" | custom-call | flops 2415919104 | bytes 1048576 | tf_op jit(solution)/shard_map/own_backward/pallas_call | solution.py:584
  83.5 5.3 %collective-permute-done.10.refs_7_ = bf16[4,48,128]{2,1,0:T(8,128)(2,1)S(1)} collective-permute-done((bf16[4,48,128]{2,1,0:T(8,128)(2,1)S(1)}, bf16[4,48,128]{2,1,0:T(8,128)(2,1)S(1)}, u32[]{:S(2)}, u32[]{:S(2)}) %collective-permute-start.10) | collective-permute-done | bytes 49184 | tf_op jit(solution)/shard_map/ppermute | solution.py:714
  88.8 1.3 %finish.1 = (f32[8,32,128]{2,1,0:T(8,128)}, f32[2,2,3,2,32]{4,3,2,1,0:T(2,128)}) custom-call(s32[2,2,2]{2,1,0:T(2,128)S(1)} %copy-done.2, f32[32,32,128]{2,1,0:T(8,128)S(1)} %get-tuple-element.54.rest_ref.refs_1_, f32[32,128]{1,0:T(8,128)S(1)} %get-tuple-element.55.rlines_ref.refs_2_, bf16[16,48,128]{2,1,0:T(8,128)(2,1)S(1)} %collective-permute-done.6.zlo.refs_3_, ...), custom_call_target="tpu_custom_call" | custom-call | bytes 1048576 | tf_op jit(solution)/shard_map/finish/pallas_call | solution.py:584
  (24 shorter events, 0.1 us)
Async XLA Ops:
  2.4 10.6 %collective-permute-start = (bf16[4,48,128]{2,1,0:T(8,128)(2,1)}, bf16[4,48,128]{2,1,0:T(8,128)(2,1)S(1)}, u32[]{:S(2)}, u32[]{:S(2)}) collective-permute-start(bf16[4,48,128]{2,1,0:T(8,128)(2,1)} %get-tuple-element.41), channel_id=1, source_target_pairs={{0,16},{16,32},{32,48},{48,64},{64,80},{80,96},{96,112},{112,128},... | collective-permute-start | bytes 147464 | tf_op jit(solution)/shard_map/ppermute | solution.py:714
  4.4 8.6 %collective-permute-start.1 = (bf16[4,48,128]{2,1,0:T(8,128)(2,1)}, bf16[4,48,128]{2,1,0:T(8,128)(2,1)S(1)}, u32[]{:S(2)}, u32[]{:S(2)}) collective-permute-start(bf16[4,48,128]{2,1,0:T(8,128)(2,1)} %get-tuple-element.42), channel_id=1, source_target_pairs={{16,0},{32,16},{48,32},{64,48},{80,64},{96,80},{112,96},{128,112},... | collective-permute-start | bytes 147464 | tf_op jit(solution)/shard_map/ppermute | solution.py:714
  10.1 0.9 copy-start
  11.0 0.7 copy-start.5
  13.0 8.7 %collective-permute-start.3 = (bf16[8,48,128]{2,1,0:T(8,128)(2,1)S(1)}, bf16[8,48,128]{2,1,0:T(8,128)(2,1)S(1)}, u32[]{:S(2)}, u32[]{:S(2)}) collective-permute-start(bf16[8,48,128]{2,1,0:T(8,128)(2,1)S(1)} %get-tuple-element.46), channel_id=1, source_target_pairs={{4,0},{8,4},{12,8},{0,12},{5,1},{9,5},{13,9},{1,13},{6,2},{10,6},{... | collective-permute-start | bytes 294920 | tf_op jit(solution)/shard_map/ppermute | solution.py:714
  15.9 5.8 %collective-permute-start.2 = (bf16[8,48,128]{2,1,0:T(8,128)(2,1)S(1)}, bf16[8,48,128]{2,1,0:T(8,128)(2,1)S(1)}, u32[]{:S(2)}, u32[]{:S(2)}) collective-permute-start(bf16[8,48,128]{2,1,0:T(8,128)(2,1)S(1)} %get-tuple-element.45), channel_id=1, source_target_pairs={{0,4},{4,8},{8,12},{12,0},{1,5},{5,9},{9,13},{13,1},{2,6},{6,10},{... | collective-permute-start | bytes 294920 | tf_op jit(solution)/shard_map/ppermute | solution.py:714
  21.7 9.1 %collective-permute-start.5 = (bf16[16,48,128]{2,1,0:T(8,128)(2,1)S(1)}, bf16[16,48,128]{2,1,0:T(8,128)(2,1)S(1)}, u32[]{:S(2)}, u32[]{:S(2)}) collective-permute-start(bf16[16,48,128]{2,1,0:T(8,128)(2,1)S(1)} %get-tuple-element.51), channel_id=1, source_target_pairs={{1,0},{2,1},{3,2},{5,4},{6,5},{7,6},{9,8},{10,9},{11,10},{13,12},{... | collective-permute-start | bytes 589832 | tf_op jit(solution)/shard_map/ppermute | solution.py:714
  23.7 7.2 %copy-start.1 = (bf16[8,48,128]{2,1,0:T(8,128)(2,1)S(1)}, bf16[8,48,128]{2,1,0:T(8,128)(2,1)}, u32[]{:S(2)}) copy-start(bf16[8,48,128]{2,1,0:T(8,128)(2,1)} %get-tuple-element.70.own_ref.own.refs_2_) | copy-start | bytes 294916
  23.7 7.2 %copy-start.2 = (s32[2,2,2]{2,1,0:T(2,128)S(1)}, s32[2,2,2]{2,1,0:T(2,128)}, u32[]{:S(2)}) copy-start(s32[2,2,2]{2,1,0:T(2,128)} %refs_0_.3) | copy-start | bytes 100
  23.7 7.2 %copy-start.3 = (bf16[5,128,128]{2,1,0:T(8,128)(2,1)S(1)}, bf16[5,128,128]{2,1,0:T(8,128)(2,1)}, u32[]{:S(2)}) copy-start(bf16[5,128,128]{2,1,0:T(8,128)(2,1)} %refs_15_.1) | copy-start | bytes 491524
  23.7 7.2 %copy-start.4 = (bf16[128,128]{1,0:T(8,128)(2,1)S(1)}, bf16[128,128]{1,0:T(8,128)(2,1)}, u32[]{:S(2)}) copy-start(bf16[128,128]{1,0:T(8,128)(2,1)} %refs_14_.1) | copy-start | bytes 98308
  23.7 7.2 %copy-start.6 = (f32[8,3,128]{2,0,1:T(8,128)S(1)}, f32[8,3,128]{2,0,1:T(8,128)}, u32[]{:S(2)}) copy-start(f32[8,3,128]{2,0,1:T(8,128)} %param.12) | copy-start | bytes 36868
  23.7 7.2 %copy-start.7 = (s32[2,2,2,32]{3,2,1,0:T(2,128)S(1)}, s32[2,2,2,32]{3,2,1,0:T(2,128)}, u32[]{:S(2)}) copy-start(s32[2,2,2,32]{3,2,1,0:T(2,128)} %param.11) | copy-start | bytes 3076
  23.7 7.2 %copy-start.8 = (f32[5,128]{1,0:T(8,128)S(1)}, f32[5,128]{1,0:T(8,128)}, u32[]{:S(2)}) copy-start(f32[5,128]{1,0:T(8,128)} %refs_16_.1) | copy-start | bytes 7684
  23.7 7.1 %collective-permute-start.4 = (bf16[16,48,128]{2,1,0:T(8,128)(2,1)S(1)}, bf16[16,48,128]{2,1,0:T(8,128)(2,1)S(1)}, u32[]{:S(2)}, u32[]{:S(2)}) collective-permute-start(bf16[16,48,128]{2,1,0:T(8,128)(2,1)S(1)} %get-tuple-element.50), channel_id=1, source_target_pairs={{0,1},{1,2},{2,3},{4,5},{5,6},{6,7},{8,9},{9,10},{10,11},{12,13},{... | collective-permute-start | bytes 589832 | tf_op jit(solution)/shard_map/ppermute | solution.py:714
  59.5 10.1 %collective-permute-start.6 = (bf16[16,48,128]{2,1,0:T(8,128)(2,1)S(1)}, bf16[16,48,128]{2,1,0:T(8,128)(2,1)S(1)}, u32[]{:S(2)}, u32[]{:S(2)}) collective-permute-start(bf16[16,48,128]{2,1,0:T(8,128)(2,1)S(1)} %get-tuple-element.56), channel_id=1, source_target_pairs={{0,1},{1,2},{2,3},{4,5},{5,6},{6,7},{8,9},{9,10},{10,11},{12,13},{... | collective-permute-start | bytes 589832 | tf_op jit(solution)/shard_map/ppermute | solution.py:714
  61.4 8.2 %collective-permute-start.7 = (bf16[16,48,128]{2,1,0:T(8,128)(2,1)S(1)}, bf16[16,48,128]{2,1,0:T(8,128)(2,1)S(1)}, u32[]{:S(2)}, u32[]{:S(2)}) collective-permute-start(bf16[16,48,128]{2,1,0:T(8,128)(2,1)S(1)} %get-tuple-element.57), channel_id=1, source_target_pairs={{1,0},{2,1},{3,2},{5,4},{6,5},{7,6},{9,8},{10,9},{11,10},{13,12},{... | collective-permute-start | bytes 589832 | tf_op jit(solution)/shard_map/ppermute | solution.py:714
  69.7 6.2 %collective-permute-start.9 = (bf16[8,48,128]{2,1,0:T(8,128)(2,1)S(1)}, bf16[8,48,128]{2,1,0:T(8,128)(2,1)S(1)}, u32[]{:S(2)}, u32[]{:S(2)}) collective-permute-start(bf16[8,48,128]{2,1,0:T(8,128)(2,1)S(1)} %get-tuple-element.63), channel_id=1, source_target_pairs={{4,0},{8,4},{12,8},{0,12},{5,1},{9,5},{13,9},{1,13},{6,2},{10,6},{... | collective-permute-start | bytes 294920 | tf_op jit(solution)/shard_map/ppermute | solution.py:714
  69.8 6.1 %collective-permute-start.8 = (bf16[8,48,128]{2,1,0:T(8,128)(2,1)S(1)}, bf16[8,48,128]{2,1,0:T(8,128)(2,1)S(1)}, u32[]{:S(2)}, u32[]{:S(2)}) collective-permute-start(bf16[8,48,128]{2,1,0:T(8,128)(2,1)S(1)} %get-tuple-element.62), channel_id=1, source_target_pairs={{0,4},{4,8},{8,12},{12,0},{1,5},{5,9},{9,13},{13,1},{2,6},{6,10},{... | collective-permute-start | bytes 294920 | tf_op jit(solution)/shard_map/ppermute | solution.py:714
  76.0 12.8 %collective-permute-start.11 = (bf16[4,48,128]{2,1,0:T(8,128)(2,1)S(1)}, bf16[4,48,128]{2,1,0:T(8,128)(2,1)S(1)}, u32[]{:S(2)}, u32[]{:S(2)}) collective-permute-start(bf16[4,48,128]{2,1,0:T(8,128)(2,1)S(1)} %get-tuple-element.69), channel_id=1, source_target_pairs={{16,0},{32,16},{48,32},{64,48},{80,64},{96,80},{112,96},{128,112},... | collective-permute-start | bytes 147464 | tf_op jit(solution)/shard_map/ppermute | solution.py:714
  81.1 7.7 %collective-permute-start.10 = (bf16[4,48,128]{2,1,0:T(8,128)(2,1)S(1)}, bf16[4,48,128]{2,1,0:T(8,128)(2,1)S(1)}, u32[]{:S(2)}, u32[]{:S(2)}) collective-permute-start(bf16[4,48,128]{2,1,0:T(8,128)(2,1)S(1)} %get-tuple-element.68), channel_id=1, source_target_pairs={{0,16},{16,32},{32,48},{48,64},{64,80},{80,96},{96,112},{112,128},... | collective-permute-start | bytes 147464 | tf_op jit(solution)/shard_map/ppermute | solution.py:714
